TPU v7x, 512 devices: a whole 4x4x16 slice. The times are simulated.
512 devices in a mesh: node: 8 (over z_hi, core), dp: 64 (over y, x, z_lo).
Axes of the slice: x: 4, y: 4, z: 16 (z_hi: 4, z_lo: 4; z = z_hi * 4 + z_lo), core: 2. Of those that a mesh axis runs over, the one named last changes fastest.
Arguments:
- inputs: bfloat16 [393216, 896], P(('node', 'dp')), may hold values from -24 to 24
- cotangent: bfloat16 [393216, 1152], P(('node', 'dp')), may hold values from -6 to 6
- weight: bfloat16 [896, 1152], P('node'), may hold values from -0.1875 to 0.1875
- moment_one: float32 [1032192], P(('node', 'dp')), may hold values from -0.0068359375 to 0.0068359375
- moment_two: float32 [1032192], P(('node', 'dp')), may hold values from 2.5431316e-07 to 2.5431316e-06
Outputs:
- grad_in: bfloat16 [393216, 896], P(('node', 'dp'))
- update: float32 [1032192], P(('node', 'dp'))
- new_weight: bfloat16 [896, 1152], P('node')
All inputs are finite; a program needn't handle non-finite values.
Results may differ from a plain program's by a relative error of at most 0.007.
Values may be sent and summed in bfloat16 or wider, within the bound.
No kernel may reach another device: no remote copies, remote signals or barrier semaphores. Data moves between devices by JAX's collectives and lax.ppermute only.
A program may use at most 64 MiB of HBM per device.

v0:
```python
import jax
import jax.numpy as jnp
from jax import lax
from jax.sharding import PartitionSpec as P

STEP = 10


def shards(inputs, cotangent, weight, moment_one, moment_two):
    grad_in = jnp.einsum(
        "tq,rq->tr",
        cotangent,
        lax.all_gather(weight, "node", axis=0, tiled=True),
        preferred_element_type=jnp.float32,
    ).astype(jnp.bfloat16)
    scale = 1.0 / (inputs.shape[0] * lax.axis_size("node") * lax.axis_size("dp"))
    node_sum = lax.psum_scatter(
        jnp.einsum("td,tq->dq", inputs, cotangent, preferred_element_type=jnp.float32).astype(
            jnp.bfloat16
        ),
        "node",
        scatter_dimension=0,
        tiled=True,
    ).astype(jnp.float32)
    flattened = node_sum.reshape(-1)
    owned = lax.psum_scatter(flattened, "dp", scatter_dimension=0, tiled=True)
    gradient = owned * scale
    own_length = gradient.shape[0]
    current = lax.dynamic_slice_in_dim(
        weight.reshape(-1), lax.axis_index("dp") * own_length, own_length, 0
    ).astype(jnp.float32)
    first = 0.9 * moment_one + 0.1 * gradient
    second = 0.95 * moment_two + 0.05 * gradient * gradient
    update = first / (1.0 - 0.9**STEP) / (jnp.sqrt(second / (1.0 - 0.95**STEP)) + 1e-08)
    stepped = (current - 0.005 * (update + 0.1 * current)).astype(jnp.bfloat16)
    new_weight = lax.all_gather(stepped, "dp", axis=0, tiled=True).reshape(weight.shape)
    return (grad_in, update, new_weight)


def solution(mesh):
    return jax.shard_map(
        shards,
        mesh=mesh,
        in_specs=(
            P(("node", "dp"), None),
            P(("node", "dp"), None),
            P("node", None),
            P(("node", "dp")),
            P(("node", "dp")),
        ),
        out_specs=(P(("node", "dp"), None), P(("node", "dp")), P("node", None)),
        check_vma=False,
    )
```

profile of v0, /device:TPU:1, one launch (start us, length us, event | category | flops | bytes accessed | tf_op | source)
XLA Modules:
  0.0 1516.8 jit_solution(4605989948395983393)
XLA Ops:
  7.2 0.0 copy-start
  7.2 0.0 reduce-scatter.2.cloned.1.call-start
  7.2 1.4 copy-done
  8.6 4.7 convolution_convert_fusion
  13.3 0.0 reduce-scatter.2.cloned.1.call-update
  13.3 0.0 all-reduce.7.cloned.1.call-start
  13.4 75.1 %reduce-scatter.2.cloned.1.call-done = bf16[112,1152]{1,0:T(8,128)(2,1)} async-done(((bf16[896,1152]{1,0:T(8,128)(2,1)}), bf16[112,1152]{1,0:T(8,128)(2,1)}) %reduce-scatter.2.cloned.1.call-update) | async-done | bytes 258064 | tf_op jit(solution)/shard_map/reduce_scatter | solution.py:17
  88.5 2.0 reshape.23
  90.5 0.0 all-reduce.7.cloned.1.call-update
  90.5 0.0 all-gather.2.cloned.1.call-start
  90.5 0.7 all-gather.2.cloned.1.call-update
  91.2 0.0 all-reduce.5.cloned.1.call-start
  91.3 0.3 reshape.20
  91.6 0.0 copy-done.5
  91.6 0.6 fusion.3
  93.5 668.6 %all-reduce.7.cloned.1.call-done = f32[129024]{0:T(1024)} async-done(((f32[129024]{0:T(1024)}), f32[129024]{0:T(1024)}) %all-reduce.7.cloned.1.call-update) | async-done | bytes 516112
  762.2 1.4 fusion.2
  763.6 0.3 dynamic-update-slice
  763.9 0.7 copy-done.1
  764.6 0.0 all-reduce.5.cloned.1.call-update
  764.6 106.9 %all-gather.2.cloned.1.call-done = bf16[896,1152]{1,0:T(8,128)(2,1)} async-done(((bf16[112,1152]{1,0:T(8,128)(2,1)}), bf16[896,1152]{1,0:T(8,128)(2,1)}) %all-gather.2.cloned.1.call-update) | async-done | bytes 2064400 | tf_op jit(solution)/shard_map/all_gather | solution.py:13
  871.5 4.8 convolution_convert_fusion.1
  876.4 632.0 %all-reduce.5.cloned.1.call-done = bf16[129024]{0:T(1024)(128)(2,1)} async-done(((bf16[129024]{0:T(1024)(128)(2,1)}), bf16[129024]{0:T(1024)(128)(2,1)}) %all-reduce.5.cloned.1.call-update) | async-done | bytes 258064
  1508.3 2.0 reshape.21
  (9 shorter events, 0.0 us)
Async XLA Ops:
  7.2 1.5 copy-start
  7.2 81.3 %reduce-scatter.2.cloned.1.call-start = ((), (), s32[]{:S(2)}) async-start(), calls=%async_computation.2 | async-start | bytes 2322432 | tf_op jit(solution)/shard_map/reduce_scatter | solution.py:17
  13.3 78.0 %copy-start.2 = (bf16[112,1152]{1,0:T(8,128)(2,1)S(1)}, bf16[112,1152]{1,0:T(8,128)(2,1)}, u32[]{:S(2)}) copy-start(bf16[112,1152]{1,0:T(8,128)(2,1)} %param.7) | copy-start | bytes 774148
  13.3 78.3 %copy-start.5 = (u32[512]{0:T(512)S(1)}, u32[512]{0:T(512)}, u32[]{:S(2)}) copy-start(u32[512]{0:T(512)} %constant.39) | copy-start | bytes 6148
  13.3 748.8 %copy-start.3 = (f32[2016]{0:T(1024)S(1)}, f32[2016]{0:T(1024)}, u32[]{:S(2)}) copy-start(f32[2016]{0:T(1024)} %param.9) | copy-start | bytes 24196
  13.3 748.8 %copy-start.4 = (f32[2016]{0:T(1024)S(1)}, f32[2016]{0:T(1024)}, u32[]{:S(2)}) copy-start(f32[2016]{0:T(1024)} %param.8) | copy-start | bytes 24196
  13.3 748.8 %all-reduce.7.cloned.1.call-start = ((), (), s32[]{:S(2)}) async-start(), calls=%async_computation.4 | async-start | bytes 1032192
  90.5 781.1 %all-gather.2.cloned.1.call-start = ((), (), s32[]{:S(2)}) async-start(), calls=%async_computation.1 | async-start | bytes 2322432 | tf_op jit(solution)/shard_map/all_gather | solution.py:13
  91.2 1417.1 %all-reduce.5.cloned.1.call-start = ((), (), s32[]{:S(2)}) async-start(), calls=%async_computation.3 | async-start | bytes 516096
  763.9 0.7 copy-start.1
Sparse Core Ops, SparseCore 0:
  13.5 74.9 reduce-scatter.1
  91.9 670.1 all-reduce.6
  764.5 106.9 all-gather.1
  875.1 633.1 all-reduce.4
where the time goes:
time: 1540 us; the launch traced here: 1520 us
  waiting for transfers between devices  1480 us (96%)
    unnamed x6, waiting for transfers between devices  1300 us
    all_gather x1, waiting for transfers between devices, shards(): lax.all_gather(weight, 'node', axis=0, tiled=True)  107 us
    reduce_scatter x1, waiting for transfers between devices, shards(): lax.psum_scatter(jnp.einsum('td,tq->dq', inputs, cotangent, preferred_ele...  75.1 us
  transfers between devices with their start and end apart: 4, of which 4 were waited for; matrix products, arithmetic and copies ran while one was open for 0% of the time, Pallas kernels for 0%

commit v1 on v0

v1 whole, which is shorter than its diff:
```python
import jax
import jax.numpy as jnp
import numpy as np
from jax import lax
from jax.sharding import Mesh, PartitionSpec as P

STEP = 10
AXES = ("zh", "core", "y", "x", "zl")
SIZES = (4, 2, 4, 4, 4)


def selection():
    pick = np.zeros((2, 16, 4, 8, 896), np.float32)
    for core in range(2):
        for yx in range(16):
            for zh in range(4):
                for r in range(7):
                    pick[core, yx, zh, r, zh * 224 + core * 112 + yx * 7 + r] = 1.0
    return pick.reshape(1024, 896)


def shards(inputs, cotangent, weight, moment_one, moment_two):
    bf16, f32 = jnp.bfloat16, jnp.float32
    core = lax.axis_index("core")
    turned = jnp.einsum(
        "pr,tr->pt", jnp.asarray(selection(), bf16), inputs, preferred_element_type=f32
    ).astype(bf16).reshape(2, 512, 768)
    theirs = lax.dynamic_index_in_dim(turned, 1 - core, 0, keepdims=False)
    mine = lax.dynamic_index_in_dim(turned, core, 0, keepdims=False)
    send = jnp.dot(theirs, cotangent, preferred_element_type=f32).astype(bf16)
    got = lax.ppermute(send, "core", [(0, 1), (1, 0)])
    kept = jnp.dot(mine, cotangent, preferred_element_type=f32).astype(bf16)
    chip = (kept.astype(f32) + got.astype(f32)).astype(bf16).reshape(16, 4, 8, 1152)
    plane = lax.all_to_all(chip, ("y", "x"), 0, 0)
    plane = jnp.sum(plane.astype(f32), axis=0)
    quarters = plane[:, :7].astype(bf16).reshape(16, 1, 2016)
    column = lax.all_to_all(quarters, ("zh", "zl"), 0, 0)
    gradient = jnp.sum(column.astype(f32), axis=0).reshape(2016) * (1.0 / 393216)

    own = (lax.axis_index("y") * 4 + lax.axis_index("x")) * 4 + lax.axis_index("zl")
    current = lax.dynamic_slice_in_dim(weight.reshape(-1), own * 2016, 2016, 0).astype(f32)
    first = 0.9 * moment_one + 0.1 * gradient
    second = 0.95 * moment_two + 0.05 * gradient * gradient
    update = first / (1.0 - 0.9**STEP) / (jnp.sqrt(second / (1.0 - 0.95**STEP)) + 1e-08)
    stepped = (current - 0.005 * (update + 0.1 * current)).astype(bf16)
    spread = jnp.broadcast_to(stepped.reshape(1, 1, 2016), (64, 1, 2016))
    new_weight = lax.all_to_all(spread, ("y", "x", "zl"), 0, 0).reshape(112, 1152)

    whole = lax.all_gather(weight, ("zh", "core"), axis=0, tiled=True)
    grad_in = jnp.einsum("tq,rq->tr", cotangent, whole, preferred_element_type=f32).astype(bf16)
    return (grad_in, update, new_weight)


def solution(mesh):
    fine = Mesh(mesh.devices.reshape(SIZES), AXES)
    return jax.shard_map(
        shards,
        mesh=fine,
        in_specs=(
            P(AXES, None),
            P(AXES, None),
            P(("zh", "core"), None),
            P(AXES),
            P(AXES),
        ),
        out_specs=(P(AXES, None), P(AXES), P(("zh", "core"), None)),
        check_vma=False,
    )
```

time: 1540 us -> 114 us (0.07); the launches traced: 1520 us -> 113 us
  waiting for transfers between devices: 1480 us -> 17 us
  blocking collectives: 0 us -> 36.8 us
  starting transfers between devices: 0.16 us -> 22 us
    unnamed x6 -> x1, waiting for transfers between devices: 1300 us -> 0.02 us
    all_gather x1, waiting for transfers between devices: 107 us -> 0.01 us  [shards(): whole = lax.all_gather(weight, ('zh', 'core'), axis=0, tiled=True)]
    reduce_scatter x1 -> x0, waiting for transfers between devices: 75.1 us -> none  [shards(): lax.psum_scatter(jnp.einsum('td,tq->dq', inputs, cotangent, preferred_ele...]
    all_to_all x0 -> x2, blocking collectives: none -> 36.8 us  [the longest x1 21.1 us: shards(): plane = lax.all_to_all(chip, ('y', 'x'), 0, 0)]
  transfers between devices with their start and end apart: 4 -> 3, of which waited for: 4 -> 2; matrix products, arithmetic and copies ran while one was open for 0% -> 11% of each run, Pallas kernels for 0% -> 0%
where the time goes in v1:
time: 114 us; the launch traced here: 113 us
  blocking collectives  36.8 us (32%)
  starting transfers between devices  22 us (19%)
  waiting for transfers between devices  17 us (15%)
  between operations  14.2 us (12%)
  matrix products  13.2 us (12%)
  other arithmetic  5.77 us (5%)
  local copies, waits for them, and re-layouts  4 us (4%)
    all_to_all x1, blocking collectives, shards(): plane = lax.all_to_all(chip, ('y', 'x'), 0, 0)  21.1 us
    all_to_all x1, blocking collectives, shards(): lax.all_to_all(spread, ('y', 'x', 'zl'), 0, 0).reshape(112, 1152)  15.7 us
    all_to_all x1, waiting for transfers between devices, shards(): column = lax.all_to_all(quarters, ('zh', 'zl'), 0, 0)  14.3 us
    all_to_all x1, starting transfers between devices, shards(): column = lax.all_to_all(quarters, ('zh', 'zl'), 0, 0)  13.2 us
    ppermute x1, starting transfers between devices, shards(): got = lax.ppermute(send, 'core', [(0, 1), (1, 0)])  8.77 us
    dot_general x1, matrix products, shards(): jnp.einsum('tq,rq->tr', cotangent, whole, preferred_element_type=f32)  4.81 us
    dot_general x1, matrix products, shards(): jnp.einsum('pr,tr->pt', jnp.asarray(selection(), bf16), inputs, preferred...  3.83 us
    ppermute x1, waiting for transfers between devices, shards(): got = lax.ppermute(send, 'core', [(0, 1), (1, 0)])  2.64 us
  transfers between devices with their start and end apart: 3, of which 2 were waited for; matrix products, arithmetic and copies ran while one was open for 11% of the time, Pallas kernels for 0%

profile of v1, /device:TPU:1, one launch (start us, length us, event | category | flops | bytes accessed | tf_op | source)
XLA Modules:
  0.0 112.9 jit_solution(8894861561101152094)
XLA Ops:
  7.2 3.8 %convolution_convert_fusion.2 = bf16[1024,768]{1,0:T(8,128)(2,1)S(1)} fusion(bf16[1024,896]{1,0:T(8,128)(2,1)} %constant.63.clone, bf16[768,896]{1,0:T(8,128)(2,1)} %param.6), kind=kOutput, calls=%fused_computation.4 | convolution fusion | flops 1410072576 | bytes 4784128 | tf_op jit(solution)/shard_map/pr,tr->pt/dot_general | solution.py:25
  11.1 2.2 %convolution_convert_fusion = bf16[512,1152]{1,0:T(8,128)(2,1)} fusion(bf16[768,1152]{1,0:T(8,128)(2,1)S(1)} %copy-done, bf16[2,512,768]{2,1,0:T(8,128)(2,1)S(1)} %bitcast.19, s32[]{:T(128)S(6)} %select_n.11), kind=kOutput, calls=%fused_computation | convolution fusion | flops 906559488 | bytes 3735556 | tf_op jit(solution)/shard_map/dot_general | solution.py:30
  13.3 8.8 %collective-permute-start = (bf16[512,1152]{1,0:T(8,128)(2,1)}, bf16[512,1152]{1,0:T(8,128)(2,1)S(1)}, u32[]{:S(2)}, u32[]{:S(2)}) collective-permute-start(bf16[512,1152]{1,0:T(8,128)(2,1)} %convolution_convert_fusion), channel_id=1, source_target_pairs={{0,64},{64,0},{1,65},{65,1},{2,66},{66,2},{3,67},{67,3},{4,68},{68... | collective-permute-start | bytes 3538952 | tf_op jit(solution)/shard_map/ppermute | solution.py:31
  22.1 2.6 %collective-permute-done = bf16[512,1152]{1,0:T(8,128)(2,1)S(1)} collective-permute-done((bf16[512,1152]{1,0:T(8,128)(2,1)}, bf16[512,1152]{1,0:T(8,128)(2,1)S(1)}, u32[]{:S(2)}, u32[]{:S(2)}) %collective-permute-start) | collective-permute-done | bytes 1179680 | tf_op jit(solution)/shard_map/ppermute | solution.py:31
  24.8 2.3 %add_convert_fusion = bf16[512,1152]{1,0:T(8,128)(2,1)S(1)} fusion(bf16[512,1152]{1,0:T(8,128)(2,1)S(1)} %collective-permute-done, bf16[768,1152]{1,0:T(8,128)(2,1)S(1)} %copy-done, bf16[2,512,768]{2,1,0:T(8,128)(2,1)} %bitcast.20, s32[]{:T(128)S(6)} %select_n.10), kind=kOutput, calls=%fused_computation.3 | convolution fusion | flops 908918784 | bytes 4915204 | tf_op jit(solution)/shard_map/dot_general | solution.py:32
  27.1 21.1 %all_to_all.15 = bf16[16,4,8,1152]{3,2,1,0:T(8,128)(2,1)S(1)} all-to-all(bf16[16,4,8,1152]{3,2,1,0:T(8,128)(2,1)S(1)} %bitcast.17), channel_id=1, replica_groups=mesh['zh'=4,'core'=2,'y'=4,'x'=4,'zl'=4] {'y','x'}, dimensions={0} | all-to-all | bytes 2359296 | tf_op jit(solution)/shard_map/all_to_all | solution.py:34
  48.2 0.2 reduce.1
  48.4 0.1 reshape.33
  48.5 0.5 broadcast.12
  49.1 1.0 reduce.3
  50.1 0.8 reshape.35
  50.9 13.2 %all-to-all-start.1 = ((bf16[16,2,1008]{2,1,0:T(2,128)(2,1)}), bf16[16,2,1008]{2,1,0:T(2,128)(2,1)S(1)}, u32[]{:S(2)}, u32[]{:S(2)}) async-start(bf16[16,2,1008]{2,1,0:T(2,128)(2,1)} %reshape.35), calls=%async_computation.1 | async-start | bytes 131072 | tf_op jit(solution)/shard_map/all_to_all | solution.py:37
  64.0 0.3 reshape.31
  64.4 14.3 %all-to-all-done.1 = bf16[16,2,1008]{2,1,0:T(2,128)(2,1)S(1)} async-done(((bf16[16,2,1008]{2,1,0:T(2,128)(2,1)}), bf16[16,2,1008]{2,1,0:T(2,128)(2,1)S(1)}, u32[]{:S(2)}, u32[]{:S(2)}) %all-to-all-start.1) | async-done | bytes 64544 | tf_op jit(solution)/shard_map/all_to_all | solution.py:37
  78.8 0.1 convert_reduce_fusion
  79.0 0.6 fusion.9
  79.6 0.3 broadcast_in_dim.2
  79.9 2.2 %reduce.4 = bf16[64,2016]{1,0:T(8,128)(2,1)S(1)} reduce(bf16[64,1,2016]{2,1,0:T(2,128)(2,1)S(1)} %broadcast_in_dim.2, bf16[]{:T(256)} %broadcast.12), dimensions={1}, to_apply=%broadcast_in_dim.2.reduce_sub_computation | reduce | bytes 516098 | tf_op jit(solution)/shard_map/broadcast_in_dim | solution.py:46
  82.1 0.3 reshape.37
  82.4 15.7 %all_to_all.16 = bf16[64,2,1008]{2,1,0:T(2,128)(2,1)S(1)} all-to-all(bf16[64,2,1008]{2,1,0:T(2,128)(2,1)S(1)} %reshape.37), channel_id=1, replica_groups=mesh['zh'=4,'core'=2,'y'=4,'x'=4,'zl'=4] {'y','x','zl'}, dimensions={0} | all-to-all | bytes 516096 | tf_op jit(solution)/shard_map/all_to_all | solution.py:47
  98.1 0.4 reshape.38
  98.5 1.6 %reduce.2 = bf16[64,2016]{1,0:T(8,128)(2,1)S(1)} reduce(bf16[64,1,2016]{2,1,0:T(2,128)(2,1)S(1)} %reshape.38, bf16[]{:T(256)} %constant.69), dimensions={1}, to_apply=%all_to_all.11.reduce_sub_computation | reduce | bytes 516098 | tf_op jit(solution)/shard_map/all_to_all | solution.py:47
  100.1 1.2 %reshape.32 = bf16[112,1152]{1,0:T(8,128)(2,1)} reshape(bf16[64,2016]{1,0:T(8,128)(2,1)S(1)} %reduce.2) | data formatting | bytes 516096 | tf_op jit(solution)/shard_map/reshape | solution.py:47
  101.3 4.8 %convolution_convert_fusion.3 = bf16[768,896]{1,0:T(8,128)(2,1)} fusion(bf16[768,1152]{1,0:T(8,128)(2,1)S(1)} %copy-done, bf16[896,1152]{1,0:T(8,128)(2,1)} %all-gather.2.cloned.1.call-done), kind=kOutput, calls=%fused_computation.5 | convolution fusion | flops 1586135040 | bytes 5210112 | tf_op jit(solution)/shard_map/tq,rq->tr/dot_general | solution.py:50
  (14 shorter events, 0.2 us)
Async XLA Ops:
  7.2 3.9 %copy-start = (bf16[768,1152]{1,0:T(8,128)(2,1)S(1)}, bf16[768,1152]{1,0:T(8,128)(2,1)}, u32[]{:S(2)}) copy-start(bf16[768,1152]{1,0:T(8,128)(2,1)} %param.7) | copy-start | bytes 5308420
  7.2 94.1 %all-gather.2.cloned.1.call-start = ((), (), s32[]{:S(2)}) async-start(), calls=%async_computation.3 | async-start | bytes 2322432 | tf_op jit(solution)/shard_map/all_gather | solution.py:49
  11.1 2.3 %copy-start.4 = (bf16[1024,768]{1,0:T(8,128)(2,1)}, bf16[1024,768]{1,0:T(8,128)(2,1)S(1)}, u32[]{:S(2)}) copy-start(bf16[1024,768]{1,0:T(8,128)(2,1)S(1)} %convolution_convert_fusion.2) | copy-start | bytes 4718596
  13.3 11.4 %collective-permute-start = (bf16[512,1152]{1,0:T(8,128)(2,1)}, bf16[512,1152]{1,0:T(8,128)(2,1)S(1)}, u32[]{:S(2)}, u32[]{:S(2)}) collective-permute-start(bf16[512,1152]{1,0:T(8,128)(2,1)} %convolution_convert_fusion), channel_id=1, source_target_pairs={{0,64},{64,0},{1,65},{65,1},{2,66},{66,2},{3,67},{67,3},{4,68},{68... | collective-permute-start | bytes 3538952 | tf_op jit(solution)/shard_map/ppermute | solution.py:31
  27.1 37.0 %copy-start.1 = (bf16[112,1152]{1,0:T(8,128)(2,1)S(1)}, bf16[112,1152]{1,0:T(8,128)(2,1)}, u32[]{:S(2)}) copy-start(bf16[112,1152]{1,0:T(8,128)(2,1)} %param.8) | copy-start | bytes 774148
  48.2 30.7 %copy-start.2 = (f32[2016]{0:T(1024)S(1)}, f32[2016]{0:T(1024)}, u32[]{:S(2)}) copy-start(f32[2016]{0:T(1024)} %param.10) | copy-start | bytes 24196
  48.2 30.7 %copy-start.3 = (f32[2016]{0:T(1024)S(1)}, f32[2016]{0:T(1024)}, u32[]{:S(2)}) copy-start(f32[2016]{0:T(1024)} %param.9) | copy-start | bytes 24196
  50.9 27.8 %all-to-all-start.1 = ((bf16[16,2,1008]{2,1,0:T(2,128)(2,1)}), bf16[16,2,1008]{2,1,0:T(2,128)(2,1)S(1)}, u32[]{:S(2)}, u32[]{:S(2)}) async-start(bf16[16,2,1008]{2,1,0:T(2,128)(2,1)} %reshape.35), calls=%async_computation.1 | async-start | bytes 131072 | tf_op jit(solution)/shard_map/all_to_all | solution.py:37
Sparse Core Ops, SparseCore 0:
  22.2 63.7 all-gather.1

commit v2 on v1

v2 whole, which is shorter than its diff:
```python
import jax
import jax.numpy as jnp
from jax import lax
from jax.experimental import pallas as pl
from jax.experimental.pallas import tpu as pltpu
from jax.sharding import Mesh, PartitionSpec as P

STEP = 10
AXES = ("zh", "core", "y", "x", "zl")
SIZES = (4, 2, 4, 4, 4)
BF16, F32 = jnp.bfloat16, jnp.float32
VMEM = pl.BlockSpec(memory_space=pltpu.VMEM)
SMEM = pl.BlockSpec(memory_space=pltpu.SMEM)
PARAMS = pltpu.CompilerParams(vmem_limit_bytes=40 * 1024 * 1024)


def term_kernel(half_ref, x_ref, c_ref, out_ref):
    half = half_ref[0]
    for pair in range(2):
        low = 384 * pair
        place = lax.broadcasted_iota(jnp.int32, (256, 512), 0)
        column = lax.broadcasted_iota(jnp.int32, (256, 512), 1)
        row = place & 7
        source = (2 * pair + ((place >> 3) & 1)) * 224 + half * 112 + (place >> 4) * 7 + row - low
        pick = jnp.where((source == column) & (row < 7), 1.0, 0.0).astype(BF16)
        turned = lax.dot_general(
            pick, x_ref[:, low : low + 512], (((1,), (1,)), ((), ())), preferred_element_type=F32
        ).astype(BF16)
        part = jnp.dot(turned, c_ref[...], preferred_element_type=F32).astype(BF16)
        out_ref[:, 16 * pair : 16 * pair + 16, :] = part.reshape(16, 16, 1152)


def quarters_kernel(plane_ref, tile_ref, out_ref, flat_ref):
    total = plane_ref[0].astype(F32)
    for i in range(1, 16):
        total = total + plane_ref[i].astype(F32)
    lane = lax.broadcasted_iota(jnp.int32, (16, 128), 1)
    tile = tile_ref[...]
    for zh in range(4):
        for k in range(9):
            flat_ref[zh, pl.ds(k, 8, stride=9), :] = total[8 * zh : 8 * zh + 8, 128 * k : 128 * k + 128]
        for q in range(4):
            row, off = divmod(2016 * q, 128)
            here = flat_ref[zh, row : row + 16, :]
            if off:
                after = flat_ref[zh, row + 1 : row + 17, :]
                here = jnp.where(
                    lane < 128 - off,
                    pltpu.roll(here, 128 - off, axis=1),
                    pltpu.roll(after, 128 - off, axis=1),
                )
            out_ref[4 * zh + q, 0:16, :] = here.astype(BF16)
            out_ref[4 * zh + q, 16:32, :] = tile


def step_kernel(column_ref, one_ref, two_ref, current_ref, update_ref, tiles_ref, stepped_ref):
    gradient = column_ref[0, 0:16, :].astype(F32)
    for i in range(1, 16):
        gradient = gradient + column_ref[i, 0:16, :].astype(F32)
    gradient = gradient * (1.0 / 393216)
    current = current_ref[...]
    first = 0.9 * one_ref[...] + 0.1 * gradient
    second = 0.95 * two_ref[...] + 0.05 * gradient * gradient
    update = first / (1.0 - 0.9**STEP) / (jnp.sqrt(second / (1.0 - 0.95**STEP)) + 1e-08)
    update_ref[...] = update
    stepped = (current - 0.005 * (update + 0.1 * current)).astype(BF16)
    for i in range(64):
        stepped_ref[i] = stepped
    for z in range(16):
        tile = column_ref[z, 16:32, :]
        for i in range(16):
            tiles_ref[i, z] = tile


def rows_kernel(piece_ref, out_ref, flat_ref, rows_ref):
    lane = lax.broadcasted_iota(jnp.int32, (16, 128), 1)
    line = lax.broadcasted_iota(jnp.int32, (16, 128), 0)
    for p in range(16):
        for q in range(4):
            row, off = divmod(2016 * q, 128)
            piece = piece_ref[4 * p + q].astype(F32)
            if off:
                piece = pltpu.roll(piece, off, axis=1)
                above = pltpu.roll(piece, 1, axis=0)
                old = flat_ref[p, row : row + 16, :]
                flat_ref[p, row + 16 : row + 17, :] = piece[15:16, :]
                piece = jnp.where(lane >= off, piece, jnp.where(line == 0, old, above))
            flat_ref[p, row : row + 16, :] = piece
        for k in range(9):
            rows_ref[7 * p : 7 * p + 7, 128 * k : 128 * k + 128] = flat_ref[p, pl.ds(k, 7, stride=9), :]
    out_ref[...] = rows_ref[...].astype(BF16)


def input_kernel(core_ref, c_ref, own_ref, other_ref, out_ref, whole_ref):
    core = core_ref[0]
    for ref, half in ((own_ref, core), (other_ref, 1 - core)):
        for zh in range(4):
            for t in range(63):
                low = pl.multiple_of(224 * zh + 112 * half + 16 * (t // 9), 16)
                whole_ref[pl.ds(low, 16), 128 * (t % 9) : 128 * (t % 9) + 128] = ref[t // 4, 4 * zh + t % 4]
    out_ref[...] = lax.dot_general(
        c_ref[...], whole_ref[...], (((1,), (1,)), ((), ())), preferred_element_type=F32
    ).astype(BF16)


def call(kernel, outs, operands, specs, scratch=()):
    return pl.pallas_call(
        kernel,
        out_shape=outs,
        in_specs=specs,
        out_specs=jax.tree.map(lambda _: VMEM, outs),
        scratch_shapes=list(scratch),
        compiler_params=PARAMS,
    )(*operands)


def shards(inputs, cotangent, weight, moment_one, moment_two):
    shape = jax.ShapeDtypeStruct
    core = lax.axis_index("core").astype(jnp.int32).reshape(1)
    own = (lax.axis_index("y") * 4 + lax.axis_index("x")) * 4 + lax.axis_index("zl")

    def term(half):
        return call(term_kernel, shape((16, 32, 1152), BF16), (half, inputs, cotangent), [SMEM, VMEM, VMEM])

    send = term(1 - core)
    got = lax.ppermute(send, "core", [(0, 1), (1, 0)])
    kept = term(core)
    chip = (kept.astype(F32) + got.astype(F32)).astype(BF16)
    plane = lax.all_to_all(chip, ("y", "x"), 0, 0)

    own_tile = jnp.minimum(own, 62)
    tile = lax.dynamic_slice(weight, (16 * (own_tile // 9), 128 * (own_tile % 9)), (16, 128))
    current = lax.dynamic_slice_in_dim(weight.reshape(-1), own * 2016, 2016, 0)
    padded = [jnp.pad(a.astype(F32), (0, 32)).reshape(16, 128) for a in (moment_one, moment_two, current)]
    quarters = call(
        quarters_kernel,
        shape((16, 32, 128), BF16),
        (plane, tile),
        [VMEM, VMEM],
        [pltpu.VMEM((4, 72, 128), F32)],
    )
    column = lax.all_to_all(quarters, ("zh", "zl"), 0, 0)
    update, tiles, stepped = call(
        step_kernel,
        (shape((16, 128), F32), shape((16, 16, 16, 128), BF16), shape((64, 16, 128), BF16)),
        (column, *padded),
        [VMEM] * 4,
    )
    tiles = lax.all_to_all(tiles, ("y", "x"), 0, 0)
    stepped = lax.all_to_all(stepped, ("y", "x", "zl"), 0, 0)
    others = lax.ppermute(tiles, "core", [(0, 1), (1, 0)])
    new_weight = call(
        rows_kernel,
        shape((112, 1152), BF16),
        (stepped,),
        [VMEM],
        [pltpu.VMEM((16, 72, 128), F32), pltpu.VMEM((112, 1152), F32)],
    )
    grad_in = call(
        input_kernel,
        shape((768, 896), BF16),
        (core, cotangent, tiles, others),
        [SMEM, VMEM, VMEM, VMEM],
        [pltpu.VMEM((896, 1152), BF16)],
    )
    return (grad_in, update.reshape(2048)[:2016], new_weight)


def solution(mesh):
    fine = Mesh(mesh.devices.reshape(SIZES), AXES)
    return jax.shard_map(
        shards,
        mesh=fine,
        in_specs=(
            P(AXES, None),
            P(AXES, None),
            P(("zh", "core"), None),
            P(AXES),
            P(AXES),
        ),
        out_specs=(P(AXES, None), P(AXES), P(("zh", "core"), None)),
        check_vma=False,
    )
```

time: 114 us -> 114 us (level)
  waiting for transfers between devices: 17 us -> 31.5 us
  between operations: 14.2 us -> 0.8 us
  matrix products: 13.2 us -> 0 us
  Pallas kernels: 0 us -> 9.65 us
  starting transfers between devices: 22 us -> 30.6 us
  other arithmetic: 5.77 us -> 1.31 us
    all_to_all x0 -> x1, waiting for transfers between devices: none -> 19.1 us  [shards(): plane = lax.all_to_all(chip, ('y', 'x'), 0, 0)]
    dot_general x4 -> x0, matrix products: 13.2 us -> none  [the longest x1 4.81 us: shards(): jnp.einsum('tq,rq->tr', cotangent, whole, preferred_element_type=f32)]
    pallas_call x0 -> x6, Pallas kernels: none -> 9.65 us  [call(): pl.pallas_call(kernel, out_shape=outs, in_specs=specs, out_specs=jax.tree...]
    ppermute x0 -> x1, starting transfers between devices: none -> 6.72 us  [shards(): others = lax.ppermute(tiles, 'core', [(0, 1), (1, 0)])]
    all_to_all x0 -> x1, starting transfers between devices: none -> 3.83 us  [shards(): plane = lax.all_to_all(chip, ('y', 'x'), 0, 0)]
    all_to_all x1, waiting for transfers between devices: 14.3 us -> 11.6 us  [shards(): column = lax.all_to_all(quarters, ('zh', 'zl'), 0, 0)]
    broadcast_in_dim x1 -> x0, other arithmetic: 2.23 us -> none  [shards(): spread = jnp.broadcast_to(stepped.reshape(1, 1, 2016), (64, 1, 2016))]
    ppermute x1, waiting for transfers between devices: 2.64 us -> 0.74 us  [shards(): got = lax.ppermute(send, 'core', [(0, 1), (1, 0)])]
  transfers between devices with their start and end apart: 3 -> 4, of which waited for: 2 -> 3; matrix products, arithmetic and copies ran while one was open for 11% -> 0% of each run, Pallas kernels for 0% -> 2%
where the time goes in v2:
time: 114 us
  blocking collectives  36.8 us (32%)
  waiting for transfers between devices  31.5 us (28%)
  starting transfers between devices  30.6 us (27%)
  Pallas kernels  9.65 us (8%)
  local copies, waits for them, and re-layouts  3.22 us (3%)
  other arithmetic  1.31 us (1%)
    all_to_all x1, waiting for transfers between devices, shards(): plane = lax.all_to_all(chip, ('y', 'x'), 0, 0)  19.1 us
    all_to_all x1, blocking collectives, shards(): stepped = lax.all_to_all(stepped, ('y', 'x', 'zl'), 0, 0)  18.9 us
    all_to_all x1, blocking collectives, shards(): tiles = lax.all_to_all(tiles, ('y', 'x'), 0, 0)  17.9 us
    all_to_all x1, waiting for transfers between devices, shards(): column = lax.all_to_all(quarters, ('zh', 'zl'), 0, 0)  11.6 us
    all_to_all x1, starting transfers between devices, shards(): column = lax.all_to_all(quarters, ('zh', 'zl'), 0, 0)  11.3 us
    pallas_call x6, Pallas kernels, call(): pl.pallas_call(kernel, out_shape=outs, in_specs=specs, out_specs=jax.tree...  9.65 us
    ppermute x1, starting transfers between devices, shards(): got = lax.ppermute(send, 'core', [(0, 1), (1, 0)])  8.79 us
    ppermute x1, starting transfers between devices, shards(): others = lax.ppermute(tiles, 'core', [(0, 1), (1, 0)])  6.72 us
  transfers between devices with their start and end apart: 4, of which 3 were waited for; matrix products, arithmetic and copies ran while one was open for 0% of the time, Pallas kernels for 2%

profile of v2, /device:TPU:1, one launch (start us, length us, event | category | flops | bytes accessed | tf_op | source)
XLA Modules:
  0.0 113.9 jit_solution(1206836851842527248)
XLA Ops:
  0.6 1.5 %copy-done = bf16[768,1152]{1,0:T(8,128)(2,1)S(1)} copy-done((bf16[768,1152]{1,0:T(8,128)(2,1)S(1)}, bf16[768,1152]{1,0:T(8,128)(2,1)}, u32[]{:S(2)}) %copy-start) | copy-done | bytes 1769496
  2.1 1.3 %copy-done.2 = bf16[768,896]{1,0:T(8,128)(2,1)S(1)} copy-done((bf16[768,896]{1,0:T(8,128)(2,1)S(1)}, bf16[768,896]{1,0:T(8,128)(2,1)}, u32[]{:S(2)}) %copy-start.2) | copy-done | bytes 1376280
  3.5 1.7 %shard_map.77 = bf16[16,32,1152]{2,1,0:T(8,128)(2,1)S(1)} custom-call(s32[1]{0:T(128)S(6)} %sub.7.half_ref, bf16[768,896]{1,0:T(8,128)(2,1)S(1)} %copy-done.2, bf16[768,1152]{1,0:T(8,128)(2,1)S(1)} %copy-done), custom_call_target="tpu_custom_call" | custom-call | tf_op jit(solution)/shard_map/pallas_call | solution.py:107
  5.2 8.8 %collective-permute-start = (bf16[16,32,1152]{2,1,0:T(8,128)(2,1)S(1)}, bf16[16,32,1152]{2,1,0:T(8,128)(2,1)S(1)}, u32[]{:S(2)}, u32[]{:S(2)}) collective-permute-start(bf16[16,32,1152]{2,1,0:T(8,128)(2,1)S(1)} %shard_map.77), channel_id=1, source_target_pairs={{0,64},{64,0},{1,65},{65,1},{2,66},{66,2},{3,67},{67,3},{4,68},{68... | collective-permute-start | bytes 3538952 | tf_op jit(solution)/shard_map/ppermute | solution.py:126
  13.9 0.0 copy-done.1
  14.0 1.7 %shard_map.76 = bf16[16,32,1152]{2,1,0:T(8,128)(2,1)S(1)} custom-call(s32[1]{0:T(128)} %bitcast.half_ref.core_ref, bf16[768,896]{1,0:T(8,128)(2,1)S(1)} %copy-done.2, bf16[768,1152]{1,0:T(8,128)(2,1)S(1)} %copy-done.1), custom_call_target="tpu_custom_call" | custom-call | tf_op jit(solution)/shard_map/pallas_call | solution.py:107
  15.7 0.7 collective-permute-done
  16.4 1.3 %add_convert_fusion = bf16[16,32,1152]{2,1,0:T(8,128)(2,1)} fusion(bf16[16,32,1152]{2,1,0:T(8,128)(2,1)S(1)} %collective-permute-done, bf16[16,32,1152]{2,1,0:T(8,128)(2,1)S(1)} %shard_map.76), kind=kLoop, calls=%fused_computation | loop fusion | flops 2359296 | bytes 3538944 | tf_op jit(solution)/shard_map/convert_element_type | solution.py:128
  17.7 3.8 %all-to-all-start = ((bf16[16,32,1152]{2,1,0:T(8,128)(2,1)}), bf16[16,32,1152]{2,1,0:T(8,128)(2,1)S(1)}, u32[]{:S(2)}, u32[]{:S(2)}) async-start(bf16[16,32,1152]{2,1,0:T(8,128)(2,1)} %add_convert_fusion), calls=%async_computation | async-start | bytes 2359296 | tf_op jit(solution)/shard_map/all_to_all | solution.py:129
  21.5 0.0 copy-start.4
  21.6 0.0 copy-start.5
  21.6 19.1 %all-to-all-done.plane_ref = bf16[16,32,1152]{2,1,0:T(8,128)(2,1)S(1)} async-done(((bf16[16,32,1152]{2,1,0:T(8,128)(2,1)}), bf16[16,32,1152]{2,1,0:T(8,128)(2,1)S(1)}, u32[]{:S(2)}, u32[]{:S(2)}) %all-to-all-start) | async-done | bytes 1179680 | tf_op jit(solution)/shard_map/all_to_all | solution.py:129
  40.8 0.9 shard_map.78
  41.7 11.3 %all-to-all-start.1 = ((bf16[16,32,128]{2,1,0:T(8,128)(2,1)}), bf16[16,32,128]{2,1,0:T(8,128)(2,1)S(1)}, u32[]{:S(2)}, u32[]{:S(2)}) async-start(bf16[16,32,128]{2,1,0:T(8,128)(2,1)} %shard_map.78), calls=%async_computation.1 | async-start | bytes 262144 | tf_op jit(solution)/shard_map/all_to_all | solution.py:142
  53.0 0.3 reshape.29
  53.3 0.1 dynamic_slice.7
  53.4 11.6 %all-to-all-done.1.column_ref = bf16[16,32,128]{2,1,0:T(8,128)(2,1)S(1)} async-done(((bf16[16,32,128]{2,1,0:T(8,128)(2,1)}), bf16[16,32,128]{2,1,0:T(8,128)(2,1)S(1)}, u32[]{:S(2)}, u32[]{:S(2)}) %all-to-all-start.1) | async-done | bytes 131104 | tf_op jit(solution)/shard_map/all_to_all | solution.py:142
  65.0 0.8 shard_map.79
  65.8 17.9 %all_to_all.20.own_ref = bf16[16,16,16,128]{3,2,1,0:T(8,128)(2,1)S(1)} all-to-all(bf16[16,16,16,128]{3,2,1,0:T(8,128)(2,1)S(1)} %get-tuple-element.6), channel_id=1, replica_groups=mesh['zh'=4,'core'=2,'y'=4,'x'=4,'zl'=4] {'y','x'}, dimensions={0} | all-to-all | bytes 2097152 | tf_op jit(solution)/shard_map/all_to_all | solution.py:149
  83.8 6.7 %collective-permute-start.1 = (bf16[16,16,16,128]{3,2,1,0:T(8,128)(2,1)S(1)}, bf16[16,16,16,128]{3,2,1,0:T(8,128)(2,1)S(1)}, u32[]{:S(2)}, u32[]{:S(2)}) collective-permute-start(bf16[16,16,16,128]{3,2,1,0:T(8,128)(2,1)S(1)} %all_to_all.20.own_ref), channel_id=1, source_target_pairs={{0,64},{64,0},{1,65},{65,1},{2,66},{66,2},{3,67},{67,3},{4,68},{68... | collective-permute-start | bytes 3145736 | tf_op jit(solution)/shard_map/ppermute | solution.py:151
  90.5 18.9 %all_to_all.21.piece_ref = bf16[64,16,128]{2,1,0:T(8,128)(2,1)S(1)} all-to-all(bf16[64,16,128]{2,1,0:T(8,128)(2,1)S(1)} %get-tuple-element.8), channel_id=1, replica_groups=mesh['zh'=4,'core'=2,'y'=4,'x'=4,'zl'=4] {'y','x','zl'}, dimensions={0} | all-to-all | bytes 524288 | tf_op jit(solution)/shard_map/all_to_all | solution.py:150
  109.4 0.9 shard_map.81
  110.3 0.0 collective-permute-done.1.other_ref
  110.3 3.6 %shard_map.80 = bf16[768,896]{1,0:T(8,128)(2,1)} custom-call(s32[1]{0:T(128)} %bitcast.half_ref.core_ref, bf16[768,1152]{1,0:T(8,128)(2,1)S(1)} %copy-done.1, bf16[16,16,16,128]{3,2,1,0:T(8,128)(2,1)S(1)} %all_to_all.20.own_ref, bf16[16,16,16,128]{3,2,1,0:T(8,128)(2,1)S(1)} %collective-permute-done.1.other_ref), custom_call_target="tpu_custom_call" | custom-call | tf_op jit(solution)/shard_map/pallas_call | solution.py:107
  (10 shorter events, 0.0 us)
Async XLA Ops:
  0.6 1.5 %copy-start = (bf16[768,1152]{1,0:T(8,128)(2,1)S(1)}, bf16[768,1152]{1,0:T(8,128)(2,1)}, u32[]{:S(2)}) copy-start(bf16[768,1152]{1,0:T(8,128)(2,1)} %c_ref.5) | copy-start | bytes 5308420
  2.1 1.3 %copy-start.2 = (bf16[768,896]{1,0:T(8,128)(2,1)S(1)}, bf16[768,896]{1,0:T(8,128)(2,1)}, u32[]{:S(2)}) copy-start(bf16[768,896]{1,0:T(8,128)(2,1)} %x_ref.3) | copy-start | bytes 4128772
  3.5 10.5 %copy-start.1 = (bf16[768,1152]{1,0:T(8,128)(2,1)S(1)}, bf16[768,1152]{1,0:T(8,128)(2,1)}, u32[]{:S(2)}) copy-start(bf16[768,1152]{1,0:T(8,128)(2,1)} %c_ref.5) | copy-start | bytes 5308420
  5.2 11.2 %collective-permute-start = (bf16[16,32,1152]{2,1,0:T(8,128)(2,1)S(1)}, bf16[16,32,1152]{2,1,0:T(8,128)(2,1)S(1)}, u32[]{:S(2)}, u32[]{:S(2)}) collective-permute-start(bf16[16,32,1152]{2,1,0:T(8,128)(2,1)S(1)} %shard_map.77), channel_id=1, source_target_pairs={{0,64},{64,0},{1,65},{65,1},{2,66},{66,2},{3,67},{67,3},{4,68},{68... | collective-permute-start | bytes 3538952 | tf_op jit(solution)/shard_map/ppermute | solution.py:126
  17.7 3.9 %copy-start.3 = (bf16[112,1152]{1,0:T(8,128)(2,1)S(1)}, bf16[112,1152]{1,0:T(8,128)(2,1)}, u32[]{:S(2)}) copy-start(bf16[112,1152]{1,0:T(8,128)(2,1)} %param.7) | copy-start | bytes 774148
  17.7 23.1 %all-to-all-start = ((bf16[16,32,1152]{2,1,0:T(8,128)(2,1)}), bf16[16,32,1152]{2,1,0:T(8,128)(2,1)S(1)}, u32[]{:S(2)}, u32[]{:S(2)}) async-start(bf16[16,32,1152]{2,1,0:T(8,128)(2,1)} %add_convert_fusion), calls=%async_computation | async-start | bytes 2359296 | tf_op jit(solution)/shard_map/all_to_all | solution.py:129
  21.5 31.8 %copy-start.4 = (f32[2016]{0:T(1024)S(1)}, f32[2016]{0:T(1024)}, u32[]{:S(2)}) copy-start(f32[2016]{0:T(1024)} %param.9) | copy-start | bytes 24196
  21.6 31.8 %copy-start.5 = (f32[2016]{0:T(1024)S(1)}, f32[2016]{0:T(1024)}, u32[]{:S(2)}) copy-start(f32[2016]{0:T(1024)} %param.8) | copy-start | bytes 24196
  41.7 23.3 %all-to-all-start.1 = ((bf16[16,32,128]{2,1,0:T(8,128)(2,1)}), bf16[16,32,128]{2,1,0:T(8,128)(2,1)S(1)}, u32[]{:S(2)}, u32[]{:S(2)}) async-start(bf16[16,32,128]{2,1,0:T(8,128)(2,1)} %shard_map.78), calls=%async_computation.1 | async-start | bytes 262144 | tf_op jit(solution)/shard_map/all_to_all | solution.py:142
  83.8 26.6 %collective-permute-start.1 = (bf16[16,16,16,128]{3,2,1,0:T(8,128)(2,1)S(1)}, bf16[16,16,16,128]{3,2,1,0:T(8,128)(2,1)S(1)}, u32[]{:S(2)}, u32[]{:S(2)}) collective-permute-start(bf16[16,16,16,128]{3,2,1,0:T(8,128)(2,1)S(1)} %all_to_all.20.own_ref), channel_id=1, source_target_pairs={{0,64},{64,0},{1,65},{65,1},{2,66},{66,2},{3,67},{67,3},{4,68},{68... | collective-permute-start | bytes 3145736 | tf_op jit(solution)/shard_map/ppermute | solution.py:151

commit v3 on v2

v3 whole, which is shorter than its diff:
```python
import jax
import jax.numpy as jnp
from jax import lax
from jax.experimental import pallas as pl
from jax.experimental.pallas import tpu as pltpu
from jax.sharding import Mesh, PartitionSpec as P

STEP = 10
AXES = ("zh", "core", "y", "x", "zl")
SIZES = (4, 2, 4, 4, 4)
BF16, F32 = jnp.bfloat16, jnp.float32
VMEM = pl.BlockSpec(memory_space=pltpu.VMEM)
SMEM = pl.BlockSpec(memory_space=pltpu.SMEM)
PARAMS = pltpu.CompilerParams(vmem_limit_bytes=16 * 1024 * 1024)


def term_kernel(half_ref, x_ref, c_ref, out_ref):
    half = half_ref[0]
    for pair in range(2):
        low = 384 * pair
        place = lax.broadcasted_iota(jnp.int32, (256, 512), 0)
        column = lax.broadcasted_iota(jnp.int32, (256, 512), 1)
        row = place & 7
        source = (2 * pair + ((place >> 3) & 1)) * 224 + half * 112 + (place >> 4) * 7 + row - low
        pick = jnp.where((source == column) & (row < 7), 1.0, 0.0).astype(BF16)
        turned = lax.dot_general(
            pick, x_ref[:, low : low + 512], (((1,), (1,)), ((), ())), preferred_element_type=F32
        ).astype(BF16)
        part = jnp.dot(turned, c_ref[...], preferred_element_type=F32).astype(BF16)
        out_ref[:, 16 * pair : 16 * pair + 16, :] = part.reshape(16, 16, 1152)


def column_kernel(plane_ref, tile_ref, out_ref, flat_ref):
    total = plane_ref[0].astype(F32)
    for i in range(1, 16):
        total = total + plane_ref[i].astype(F32)
    tile = tile_ref[...]
    for zh in range(4):
        for k in range(9):
            flat_ref[zh, pl.ds(k, 8, stride=9), :] = total[8 * zh : 8 * zh + 8, 128 * k : 128 * k + 128]
        flat = flat_ref[zh, 0:64, :].astype(BF16)
        for zl in range(4):
            out_ref[4 * zh + zl, 0:64, :] = flat
            out_ref[4 * zh + zl, 64:80, :] = tile


def lay(flat_ref, pieces):
    lane = lax.broadcasted_iota(jnp.int32, (16, 128), 1)
    line = lax.broadcasted_iota(jnp.int32, (16, 128), 0)
    for q in range(4):
        row, off = divmod(2016 * q, 128)
        piece = pieces[q]
        if off:
            piece = pltpu.roll(piece, off, axis=1)
            above = pltpu.roll(piece, 1, axis=0)
            old = flat_ref[row : row + 16, :]
            flat_ref[row + 16 : row + 17, :] = piece[15:16, :]
            piece = jnp.where(lane >= off, piece, jnp.where(line == 0, old, above))
        flat_ref[row : row + 16, :] = piece
    return flat_ref[0:64, :]


def cut(flat_ref, q):
    lane = lax.broadcasted_iota(jnp.int32, (16, 128), 1)
    row, off = divmod(2016 * q, 128)
    here = flat_ref[row : row + 16, :]
    if off:
        after = flat_ref[row + 1 : row + 17, :]
        here = jnp.where(
            lane < 128 - off, pltpu.roll(here, 128 - off, axis=1), pltpu.roll(after, 128 - off, axis=1)
        )
    return here


def step_kernel(
    zl_ref, zh_ref, column_ref, own_ref, m1_ref, m2_ref, m3_ref, current_ref, update_ref, out_ref, quarter_ref, flat_ref
):
    zl = zl_ref[0]
    quarter_ref[zl] = own_ref[...]
    quarter_ref[zl ^ 1] = m1_ref[...]
    quarter_ref[zl ^ 2] = m2_ref[...]
    quarter_ref[zl ^ 3] = m3_ref[...]
    flat_ref[...] = jnp.zeros_like(flat_ref)
    one = lay(flat_ref.at[0], [quarter_ref[q, 0] for q in range(4)])
    two = lay(flat_ref.at[1], [quarter_ref[q, 1] for q in range(4)])
    for k in range(9):
        flat_ref[2, pl.ds(k, 8, stride=9), :] = current_ref[:, 128 * k : 128 * k + 128]
    current = flat_ref[2, 0:64, :]
    gradient = column_ref[0, 0:64, :].astype(F32)
    for i in range(1, 16):
        gradient = gradient + column_ref[i, 0:64, :].astype(F32)
    gradient = gradient * (1.0 / 393216)
    first = 0.9 * one + 0.1 * gradient
    second = 0.95 * two + 0.05 * gradient * gradient
    update = first / (1.0 - 0.9**STEP) / (jnp.sqrt(second / (1.0 - 0.95**STEP)) + 1e-08)
    stepped = (current - 0.005 * (update + 0.1 * current)).astype(BF16)
    for i in range(16):
        out_ref[i, 0:64, :] = stepped
    zh = zh_ref[0]
    for slot in range(12):
        tile = column_ref[4 * (zh ^ (slot // 4 + 1)) + slot % 4, 64:80, :]
        for i in range(16):
            out_ref[i, 64 + 16 * slot : 80 + 16 * slot, :] = tile
    flat_ref[3, 0:64, :] = update
    for q in range(4):
        quarter_ref[q, 0] = cut(flat_ref.at[3], q)
    update_ref[...] = quarter_ref[zl, 0]


def rows_kernel(piece_ref, out_ref, flat_ref, rows_ref):
    for p in range(16):
        flat_ref[p, 0:64, :] = piece_ref[p, 0:64, :].astype(F32)
        for k in range(9):
            rows_ref[7 * p : 7 * p + 7, 128 * k : 128 * k + 128] = flat_ref[p, pl.ds(k, 7, stride=9), :]
    out_ref[...] = rows_ref[...].astype(BF16)


def input_kernel(core_ref, zh_ref, c_ref, mine_ref, yours_ref, own_ref, other_ref, out_ref, whole_ref):
    core, zh = core_ref[0], zh_ref[0]
    for rows_ref, ref, half in ((mine_ref, own_ref, core), (yours_ref, other_ref, 1 - core)):
        whole_ref[pl.ds(pl.multiple_of(224 * zh + 112 * half, 16), 112), :] = rows_ref[...]
        for d in (1, 2, 3):
            for t in range(63):
                low = pl.multiple_of(224 * (zh ^ d) + 112 * half + 16 * (t // 9), 16)
                slot = 64 + 16 * (4 * (d - 1) + t % 4)
                whole_ref[pl.ds(low, 16), 128 * (t % 9) : 128 * (t % 9) + 128] = ref[t // 4, slot : slot + 16, :]
    out_ref[...] = lax.dot_general(
        c_ref[...], whole_ref[...], (((1,), (1,)), ((), ())), preferred_element_type=F32
    ).astype(BF16)


def call(kernel, outs, operands, specs, scratch=()):
    return pl.pallas_call(
        kernel,
        out_shape=outs,
        in_specs=specs,
        out_specs=jax.tree.map(lambda _: VMEM, outs),
        scratch_shapes=list(scratch),
        compiler_params=PARAMS,
    )(*operands)


def shards(inputs, cotangent, weight, moment_one, moment_two):
    shape = jax.ShapeDtypeStruct
    core = lax.axis_index("core").astype(jnp.int32).reshape(1)
    zl, zh = (lax.axis_index(a).astype(jnp.int32).reshape(1) for a in ("zl", "zh"))
    own = (lax.axis_index("y") * 4 + lax.axis_index("x")) * 4 + lax.axis_index("zl")

    def term(half):
        return call(term_kernel, shape((16, 32, 1152), BF16), (half, inputs, cotangent), [SMEM, VMEM, VMEM])

    send = term(1 - core)
    got = lax.ppermute(send, "core", [(0, 1), (1, 0)])
    kept = term(core)
    chip = (kept.astype(F32) + got.astype(F32)).astype(BF16)
    own_tile = jnp.minimum(own, 62)
    tile = lax.dynamic_slice(weight, (16 * (own_tile // 9), 128 * (own_tile % 9)), (16, 128))
    current = lax.dynamic_slice(weight, (7 * (own // 4), 0), (7, 1152))
    current = jnp.pad(current.astype(F32), ((0, 1), (0, 0)))
    moments = jnp.stack([jnp.pad(a, (0, 32)).reshape(16, 128) for a in (moment_one, moment_two)])
    moments, mine, chip = lax.optimization_barrier((moments, weight, chip))
    plane = lax.all_to_all(chip, ("y", "x"), 0, 0)
    near = [lax.ppermute(moments, "zl", [(i, i ^ d) for i in range(4)]) for d in (1, 2, 3)]
    yours = lax.ppermute(mine, "core", [(0, 1), (1, 0)])
    plane, yours, *near = lax.optimization_barrier((plane, yours, *near))
    column = call(
        column_kernel,
        shape((16, 80, 128), BF16),
        (plane, tile),
        [VMEM, VMEM],
        [pltpu.VMEM((4, 72, 128), F32)],
    )
    column = lax.all_to_all(column, ("zh", "zl"), 0, 0)
    update, spread = call(
        step_kernel,
        (shape((16, 128), F32), shape((16, 256, 128), BF16)),
        (zl, zh, column, moments, *near, current),
        [SMEM] * 2 + [VMEM] * 6,
        [pltpu.VMEM((4, 2, 16, 128), F32), pltpu.VMEM((4, 80, 128), F32)],
    )
    spread = lax.all_to_all(spread, ("y", "x"), 0, 0)
    others = lax.ppermute(spread, "core", [(0, 1), (1, 0)])
    new_weight = call(
        rows_kernel,
        shape((112, 1152), BF16),
        (spread,),
        [VMEM],
        [pltpu.VMEM((16, 72, 128), F32), pltpu.VMEM((112, 1152), F32)],
    )
    grad_in = call(
        input_kernel,
        shape((768, 896), BF16),
        (core, zh, cotangent, weight, yours, spread, others),
        [SMEM] * 2 + [VMEM] * 5,
        [pltpu.VMEM((896, 1152), BF16)],
    )
    return (grad_in, update.reshape(2048)[:2016], new_weight)


def solution(mesh):
    fine = Mesh(mesh.devices.reshape(SIZES), AXES)
    return jax.shard_map(
        shards,
        mesh=fine,
        in_specs=(
            P(AXES, None),
            P(AXES, None),
            P(("zh", "core"), None),
            P(AXES),
            P(AXES),
        ),
        out_specs=(P(AXES, None), P(AXES), P(("zh", "core"), None)),
        check_vma=False,
    )
```

time: 114 us -> 104 us (0.912)
  the two profiles are of different devices: /device:TPU:1 before, /device:TPU:33 now
where the time goes in v3:
time: 104 us; the launch traced here: 103 us
  starting transfers between devices  40.5 us (39%)
  waiting for transfers between devices  26.6 us (26%)
  blocking collectives  21.4 us (21%)
  Pallas kernels  9.61 us (9%)
  local copies, waits for them, and re-layouts  2.86 us (3%)
  other arithmetic  1.31 us (1%)
    all_to_all x1, blocking collectives, shards(): spread = lax.all_to_all(spread, ('y', 'x'), 0, 0)  21.4 us
    all_to_all x1, waiting for transfers between devices, shards(): column = lax.all_to_all(column, ('zh', 'zl'), 0, 0)  18.2 us
    all_to_all x1, starting transfers between devices, shards(): column = lax.all_to_all(column, ('zh', 'zl'), 0, 0)  14.7 us
    pallas_call x6, Pallas kernels, call(): pl.pallas_call(kernel, out_shape=outs, in_specs=specs, out_specs=jax.tree...  9.61 us
    ppermute x3, starting transfers between devices, shards(): lax.ppermute(moments, 'zl', [(i, i ^ d) for i in range(4)])  9.01 us
    all_to_all x1, starting transfers between devices, shards(): plane = lax.all_to_all(chip, ('y', 'x'), 0, 0)  6.89 us
    ppermute x1, starting transfers between devices, shards(): others = lax.ppermute(spread, 'core', [(0, 1), (1, 0)])  4.83 us
    all_to_all x1, waiting for transfers between devices, shards(): plane = lax.all_to_all(chip, ('y', 'x'), 0, 0)  3.71 us
  transfers between devices with their start and end apart: 8, of which 6 were waited for; matrix products, arithmetic and copies ran while one was open for 0% of the time, Pallas kernels for 2%

profile of v3, /device:TPU:33, one launch (start us, length us, event | category | flops | bytes accessed | tf_op | source)
XLA Modules:
  0.0 103.2 jit_solution(15604287629983562027)
XLA Ops:
  0.6 1.5 %copy-done = bf16[768,1152]{1,0:T(8,128)(2,1)S(1)} copy-done((bf16[768,1152]{1,0:T(8,128)(2,1)S(1)}, bf16[768,1152]{1,0:T(8,128)(2,1)}, u32[]{:S(2)}) %copy-start) | copy-done | bytes 1769496
  2.1 1.3 %copy-done.2 = bf16[768,896]{1,0:T(8,128)(2,1)S(1)} copy-done((bf16[768,896]{1,0:T(8,128)(2,1)S(1)}, bf16[768,896]{1,0:T(8,128)(2,1)}, u32[]{:S(2)}) %copy-start.2) | copy-done | bytes 1376280
  3.5 1.7 %shard_map.77 = bf16[16,32,1152]{2,1,0:T(8,128)(2,1)S(1)} custom-call(s32[1]{0:T(128)S(6)} %sub.10.half_ref, bf16[768,896]{1,0:T(8,128)(2,1)S(1)} %copy-done.2, bf16[768,1152]{1,0:T(8,128)(2,1)S(1)} %copy-done), custom_call_target="tpu_custom_call" | custom-call | tf_op jit(solution)/shard_map/pallas_call | solution.py:133
  5.2 2.6 %collective-permute-start = (bf16[16,32,1152]{2,1,0:T(8,128)(2,1)S(1)}, bf16[16,32,1152]{2,1,0:T(8,128)(2,1)S(1)}, u32[]{:S(2)}, u32[]{:S(2)}) collective-permute-start(bf16[16,32,1152]{2,1,0:T(8,128)(2,1)S(1)} %shard_map.77), channel_id=1, source_target_pairs={{0,64},{64,0},{1,65},{65,1},{2,66},{66,2},{3,67},{67,3},{4,68},{68... | collective-permute-start | bytes 3538952 | tf_op jit(solution)/shard_map/ppermute | solution.py:153
  7.8 1.7 %shard_map.76 = bf16[16,32,1152]{2,1,0:T(8,128)(2,1)S(1)} custom-call(s32[1]{0:T(128)} %bitcast.half_ref.core_ref, bf16[768,896]{1,0:T(8,128)(2,1)S(1)} %copy-done.2, bf16[768,1152]{1,0:T(8,128)(2,1)S(1)} %copy-done.1), custom_call_target="tpu_custom_call" | custom-call | tf_op jit(solution)/shard_map/pallas_call | solution.py:133
  9.5 0.7 collective-permute-done
  10.2 1.3 %add_convert_fusion = bf16[16,32,1152]{2,1,0:T(8,128)(2,1)} fusion(bf16[16,32,1152]{2,1,0:T(8,128)(2,1)S(1)} %collective-permute-done, bf16[16,32,1152]{2,1,0:T(8,128)(2,1)S(1)} %shard_map.76), kind=kLoop, calls=%fused_computation | loop fusion | flops 2359296 | bytes 3538944 | tf_op jit(solution)/shard_map/convert_element_type | solution.py:155
  11.5 6.9 %all-to-all-start = ((bf16[16,32,1152]{2,1,0:T(8,128)(2,1)}), bf16[16,32,1152]{2,1,0:T(8,128)(2,1)S(1)}, u32[]{:S(2)}, u32[]{:S(2)}) async-start(bf16[16,32,1152]{2,1,0:T(8,128)(2,1)} %add_convert_fusion), calls=%async_computation | async-start | bytes 2359296 | tf_op jit(solution)/shard_map/all_to_all | solution.py:162
  18.4 2.6 %collective-permute-start.1 = (bf16[112,1152]{1,0:T(8,128)(2,1)S(1)}, bf16[112,1152]{1,0:T(8,128)(2,1)S(1)}, u32[]{:S(2)}, u32[]{:S(2)}) collective-permute-start(bf16[112,1152]{1,0:T(8,128)(2,1)S(1)} %copy-done.3), channel_id=1, source_target_pairs={{0,64},{64,0},{1,65},{65,1},{2,66},{66,2},{3,67},{67,3},{4,68},{68... | collective-permute-start | bytes 774152 | tf_op jit(solution)/shard_map/ppermute | solution.py:164
  21.0 3.8 %collective-permute-start.2 = (f32[2,16,128]{2,1,0:T(8,128)S(1)}, f32[2,16,128]{2,1,0:T(8,128)S(1)}, u32[]{:S(2)}, u32[]{:S(2)}) collective-permute-start(f32[2,16,128]{2,1,0:T(8,128)S(1)} %pad_maximum_fusion.own_ref), channel_id=1, source_target_pairs={{0,1},{1,0},{2,3},{3,2},{4,5},{5,4},{6,7},{7,6},{8,9},{9,8},{10,11... | collective-permute-start | bytes 49160 | tf_op jit(solution)/shard_map/ppermute | solution.py:163
  24.8 3.1 %collective-permute-start.3 = (f32[2,16,128]{2,1,0:T(8,128)S(1)}, f32[2,16,128]{2,1,0:T(8,128)S(1)}, u32[]{:S(2)}, u32[]{:S(2)}) collective-permute-start(f32[2,16,128]{2,1,0:T(8,128)S(1)} %pad_maximum_fusion.own_ref), channel_id=1, source_target_pairs={{0,2},{1,3},{2,0},{3,1},{4,6},{5,7},{6,4},{7,5},{8,10},{9,11},{10,... | collective-permute-start | bytes 49160 | tf_op jit(solution)/shard_map/ppermute | solution.py:163
  27.9 2.2 %collective-permute-start.4 = (f32[2,16,128]{2,1,0:T(8,128)S(1)}, f32[2,16,128]{2,1,0:T(8,128)S(1)}, u32[]{:S(2)}, u32[]{:S(2)}) collective-permute-start(f32[2,16,128]{2,1,0:T(8,128)S(1)} %pad_maximum_fusion.own_ref), channel_id=1, source_target_pairs={{0,3},{1,2},{2,1},{3,0},{4,7},{5,6},{6,5},{7,4},{8,11},{9,10},{10,... | collective-permute-start | bytes 49160 | tf_op jit(solution)/shard_map/ppermute | solution.py:163
  30.1 0.4 collective-permute-done.3.m2_ref
  30.5 2.2 %collective-permute-done.4.m3_ref = f32[2,16,128]{2,1,0:T(8,128)S(1)} collective-permute-done((f32[2,16,128]{2,1,0:T(8,128)S(1)}, f32[2,16,128]{2,1,0:T(8,128)S(1)}, u32[]{:S(2)}, u32[]{:S(2)}) %collective-permute-start.4) | collective-permute-done | bytes 16416 | tf_op jit(solution)/shard_map/ppermute | solution.py:163
  32.7 3.7 %all-to-all-done.plane_ref = bf16[16,32,1152]{2,1,0:T(8,128)(2,1)S(1)} async-done(((bf16[16,32,1152]{2,1,0:T(8,128)(2,1)}), bf16[16,32,1152]{2,1,0:T(8,128)(2,1)S(1)}, u32[]{:S(2)}, u32[]{:S(2)}) %all-to-all-start) | async-done | bytes 1179680 | tf_op jit(solution)/shard_map/all_to_all | solution.py:162
  36.4 0.9 shard_map.78
  37.3 14.7 %all-to-all-start.1 = ((bf16[16,80,128]{2,1,0:T(8,128)(2,1)}), bf16[16,80,128]{2,1,0:T(8,128)(2,1)S(1)}, u32[]{:S(2)}, u32[]{:S(2)}) async-start(bf16[16,80,128]{2,1,0:T(8,128)(2,1)} %shard_map.78), calls=%async_computation.1 | async-start | bytes 655360 | tf_op jit(solution)/shard_map/all_to_all | solution.py:173
  52.0 18.2 %all-to-all-done.1.column_ref = bf16[16,80,128]{2,1,0:T(8,128)(2,1)S(1)} async-done(((bf16[16,80,128]{2,1,0:T(8,128)(2,1)}), bf16[16,80,128]{2,1,0:T(8,128)(2,1)S(1)}, u32[]{:S(2)}, u32[]{:S(2)}) %all-to-all-start.1) | async-done | bytes 327712 | tf_op jit(solution)/shard_map/all_to_all | solution.py:173
  70.2 0.9 shard_map.79
  71.1 21.4 %all_to_all.15.own_ref.piece_ref = bf16[16,256,128]{2,1,0:T(8,128)(2,1)S(1)} all-to-all(bf16[16,256,128]{2,1,0:T(8,128)(2,1)S(1)} %get-tuple-element.21), channel_id=1, replica_groups=mesh['zh'=4,'core'=2,'y'=4,'x'=4,'zl'=4] {'y','x'}, dimensions={0} | all-to-all | bytes 2097152 | tf_op jit(solution)/shard_map/all_to_all | solution.py:181
  92.5 4.8 %collective-permute-start.5 = (bf16[16,256,128]{2,1,0:T(8,128)(2,1)S(1)}, bf16[16,256,128]{2,1,0:T(8,128)(2,1)S(1)}, u32[]{:S(2)}, u32[]{:S(2)}) collective-permute-start(bf16[16,256,128]{2,1,0:T(8,128)(2,1)S(1)} %all_to_all.15.own_ref.piece_ref), channel_id=1, source_target_pairs={{0,64},{64,0},{1,65},{65,1},{2,66},{66,2},{3,67},{67,3},{4,68},{68... | collective-permute-start | bytes 3145736 | tf_op jit(solution)/shard_map/ppermute | solution.py:182
  97.4 0.9 shard_map.81
  98.2 1.4 %collective-permute-done.5.other_ref = bf16[16,256,128]{2,1,0:T(8,128)(2,1)S(1)} collective-permute-done((bf16[16,256,128]{2,1,0:T(8,128)(2,1)S(1)}, bf16[16,256,128]{2,1,0:T(8,128)(2,1)S(1)}, u32[]{:S(2)}, u32[]{:S(2)}) %collective-permute-start.5) | collective-permute-done | bytes 1048608 | tf_op jit(solution)/shard_map/ppermute | solution.py:182
  99.6 3.5 %shard_map.80 = bf16[768,896]{1,0:T(8,128)(2,1)} custom-call(s32[1]{0:T(128)} %bitcast.half_ref.core_ref, s32[1]{0:T(128)} %bitcast.1.zh_ref, bf16[768,1152]{1,0:T(8,128)(2,1)S(1)} %copy-done.1, bf16[112,1152]{1,0:T(8,128)(2,1)S(1)} %copy-done.3, bf16[112,1152]{1,0:T(8,128)(2,1)S(1)} %collective-permute-done.1.yours_ref, ...), custom_call_target="tpu_custom_call" | custom-call | tf_op jit(solution)/shard_map/pallas_call | solution.py:133
  (17 shorter events, 0.1 us)
Async XLA Ops:
  0.6 1.5 %copy-start = (bf16[768,1152]{1,0:T(8,128)(2,1)S(1)}, bf16[768,1152]{1,0:T(8,128)(2,1)}, u32[]{:S(2)}) copy-start(bf16[768,1152]{1,0:T(8,128)(2,1)} %c_ref.5) | copy-start | bytes 5308420
  2.1 1.3 %copy-start.2 = (bf16[768,896]{1,0:T(8,128)(2,1)S(1)}, bf16[768,896]{1,0:T(8,128)(2,1)}, u32[]{:S(2)}) copy-start(bf16[768,896]{1,0:T(8,128)(2,1)} %x_ref.3) | copy-start | bytes 4128772
  3.5 4.3 %copy-start.1 = (bf16[768,1152]{1,0:T(8,128)(2,1)S(1)}, bf16[768,1152]{1,0:T(8,128)(2,1)}, u32[]{:S(2)}) copy-start(bf16[768,1152]{1,0:T(8,128)(2,1)} %c_ref.5) | copy-start | bytes 5308420
  5.2 4.3 %copy-start.4 = (f32[2016]{0:T(1024)S(1)}, f32[2016]{0:T(1024)}, u32[]{:S(2)}) copy-start(f32[2016]{0:T(1024)} %param.9) | copy-start | bytes 24196
  5.2 4.3 %copy-start.5 = (f32[2016]{0:T(1024)S(1)}, f32[2016]{0:T(1024)}, u32[]{:S(2)}) copy-start(f32[2016]{0:T(1024)} %param.8) | copy-start | bytes 24196
  5.2 5.0 %collective-permute-start = (bf16[16,32,1152]{2,1,0:T(8,128)(2,1)S(1)}, bf16[16,32,1152]{2,1,0:T(8,128)(2,1)S(1)}, u32[]{:S(2)}, u32[]{:S(2)}) collective-permute-start(bf16[16,32,1152]{2,1,0:T(8,128)(2,1)S(1)} %shard_map.77), channel_id=1, source_target_pairs={{0,64},{64,0},{1,65},{65,1},{2,66},{66,2},{3,67},{67,3},{4,68},{68... | collective-permute-start | bytes 3538952 | tf_op jit(solution)/shard_map/ppermute | solution.py:153
  11.5 6.9 %copy-start.3 = (bf16[112,1152]{1,0:T(8,128)(2,1)S(1)}, bf16[112,1152]{1,0:T(8,128)(2,1)}, u32[]{:S(2)}) copy-start(bf16[112,1152]{1,0:T(8,128)(2,1)} %mine_ref.1) | copy-start | bytes 774148
  11.5 24.8 %all-to-all-start = ((bf16[16,32,1152]{2,1,0:T(8,128)(2,1)}), bf16[16,32,1152]{2,1,0:T(8,128)(2,1)S(1)}, u32[]{:S(2)}, u32[]{:S(2)}) async-start(bf16[16,32,1152]{2,1,0:T(8,128)(2,1)} %add_convert_fusion), calls=%async_computation | async-start | bytes 2359296 | tf_op jit(solution)/shard_map/all_to_all | solution.py:162
  18.4 14.2 %collective-permute-start.1 = (bf16[112,1152]{1,0:T(8,128)(2,1)S(1)}, bf16[112,1152]{1,0:T(8,128)(2,1)S(1)}, u32[]{:S(2)}, u32[]{:S(2)}) collective-permute-start(bf16[112,1152]{1,0:T(8,128)(2,1)S(1)} %copy-done.3), channel_id=1, source_target_pairs={{0,64},{64,0},{1,65},{65,1},{2,66},{66,2},{3,67},{67,3},{4,68},{68... | collective-permute-start | bytes 774152 | tf_op jit(solution)/shard_map/ppermute | solution.py:164
  21.0 9.1 %collective-permute-start.2 = (f32[2,16,128]{2,1,0:T(8,128)S(1)}, f32[2,16,128]{2,1,0:T(8,128)S(1)}, u32[]{:S(2)}, u32[]{:S(2)}) collective-permute-start(f32[2,16,128]{2,1,0:T(8,128)S(1)} %pad_maximum_fusion.own_ref), channel_id=1, source_target_pairs={{0,1},{1,0},{2,3},{3,2},{4,5},{5,4},{6,7},{7,6},{8,9},{9,8},{10,11... | collective-permute-start | bytes 49160 | tf_op jit(solution)/shard_map/ppermute | solution.py:163
  24.8 5.7 %collective-permute-start.3 = (f32[2,16,128]{2,1,0:T(8,128)S(1)}, f32[2,16,128]{2,1,0:T(8,128)S(1)}, u32[]{:S(2)}, u32[]{:S(2)}) collective-permute-start(f32[2,16,128]{2,1,0:T(8,128)S(1)} %pad_maximum_fusion.own_ref), channel_id=1, source_target_pairs={{0,2},{1,3},{2,0},{3,1},{4,6},{5,7},{6,4},{7,5},{8,10},{9,11},{10,... | collective-permute-start | bytes 49160 | tf_op jit(solution)/shard_map/ppermute | solution.py:163
  27.9 4.8 %collective-permute-start.4 = (f32[2,16,128]{2,1,0:T(8,128)S(1)}, f32[2,16,128]{2,1,0:T(8,128)S(1)}, u32[]{:S(2)}, u32[]{:S(2)}) collective-permute-start(f32[2,16,128]{2,1,0:T(8,128)S(1)} %pad_maximum_fusion.own_ref), channel_id=1, source_target_pairs={{0,3},{1,2},{2,1},{3,0},{4,7},{5,6},{6,5},{7,4},{8,11},{9,10},{10,... | collective-permute-start | bytes 49160 | tf_op jit(solution)/shard_map/ppermute | solution.py:163
  37.3 32.9 %all-to-all-start.1 = ((bf16[16,80,128]{2,1,0:T(8,128)(2,1)}), bf16[16,80,128]{2,1,0:T(8,128)(2,1)S(1)}, u32[]{:S(2)}, u32[]{:S(2)}) async-start(bf16[16,80,128]{2,1,0:T(8,128)(2,1)} %shard_map.78), calls=%async_computation.1 | async-start | bytes 655360 | tf_op jit(solution)/shard_map/all_to_all | solution.py:173
  92.5 7.1 %collective-permute-start.5 = (bf16[16,256,128]{2,1,0:T(8,128)(2,1)S(1)}, bf16[16,256,128]{2,1,0:T(8,128)(2,1)S(1)}, u32[]{:S(2)}, u32[]{:S(2)}) collective-permute-start(bf16[16,256,128]{2,1,0:T(8,128)(2,1)S(1)} %all_to_all.15.own_ref.piece_ref), channel_id=1, source_target_pairs={{0,64},{64,0},{1,65},{65,1},{2,66},{66,2},{3,67},{67,3},{4,68},{68... | collective-permute-start | bytes 3145736 | tf_op jit(solution)/shard_map/ppermute | solution.py:182

commit v4 on v3

v4 whole, which is shorter than its diff:
```python
import jax
import jax.numpy as jnp
from jax import lax
from jax.experimental import pallas as pl
from jax.experimental.pallas import tpu as pltpu
from jax.sharding import Mesh, PartitionSpec as P

STEP = 10
AXES = ("zh", "core", "y", "x", "zb", "za")
SIZES = (4, 2, 4, 4, 2, 2)
BF16, F32 = jnp.bfloat16, jnp.float32
VMEM = pl.BlockSpec(memory_space=pltpu.VMEM)
SMEM = pl.BlockSpec(memory_space=pltpu.SMEM)
PARAMS = pltpu.CompilerParams(vmem_limit_bytes=16 * 1024 * 1024)


def turn_kernel(x_ref, out_ref):
    for half in range(2):
        for pair in range(2):
            low = 384 * pair
            place = lax.broadcasted_iota(jnp.int32, (256, 512), 0)
            column = lax.broadcasted_iota(jnp.int32, (256, 512), 1)
            row = place & 7
            source = (2 * pair + ((place >> 3) & 1)) * 224 + half * 112 + (place >> 4) * 7 + row - low
            pick = jnp.where((source == column) & (row < 7), 1.0, 0.0).astype(BF16)
            out_ref[half, pair] = lax.dot_general(
                pick, x_ref[:, low : low + 512], (((1,), (1,)), ((), ())), preferred_element_type=F32
            ).astype(BF16)


def term_kernel(half_ref, turned_ref, c_ref, out_ref):
    for pair in range(2):
        part = jnp.dot(turned_ref[half_ref[0], pair], c_ref[...], preferred_element_type=F32).astype(BF16)
        out_ref[:, 16 * pair : 16 * pair + 16, :] = part.reshape(16, 16, 1152)


def add_kernel(kept_ref, got_ref, out_ref):
    for p in range(16):
        out_ref[p] = kept_ref[p] + got_ref[p]


def column_kernel(plane_ref, tile_ref, out_ref, flat_ref):
    total = plane_ref[0].astype(F32)
    for i in range(1, 16):
        total = total + plane_ref[i].astype(F32)
    tile = tile_ref[...]
    for zh in range(4):
        for k in range(9):
            flat_ref[zh, pl.ds(k, 8, stride=9), :] = total[8 * zh : 8 * zh + 8, 128 * k : 128 * k + 128]
        quarters = [cut(flat_ref.at[zh], q).astype(BF16) for q in range(4)]
        for zl in range(4):
            out_ref[4 * zh + zl, 0:16, :] = quarters[zl % 2]
            out_ref[4 * zh + zl, 16:32, :] = quarters[zl % 2 + 2]
            out_ref[4 * zh + zl, 32:48, :] = tile


def lay(flat_ref, pieces):
    lane = lax.broadcasted_iota(jnp.int32, (16, 128), 1)
    line = lax.broadcasted_iota(jnp.int32, (16, 128), 0)
    for q in range(4):
        row, off = divmod(2016 * q, 128)
        piece = pieces[q]
        if off:
            piece = pltpu.roll(piece, off, axis=1)
            above = pltpu.roll(piece, 1, axis=0)
            old = flat_ref[row : row + 16, :]
            flat_ref[row + 16 : row + 17, :] = piece[15:16, :]
            piece = jnp.where(lane >= off, piece, jnp.where(line == 0, old, above))
        flat_ref[row : row + 16, :] = piece


def cut(flat_ref, q):
    lane = lax.broadcasted_iota(jnp.int32, (16, 128), 1)
    row, off = divmod(2016 * q, 128)
    here = flat_ref[row : row + 16, :]
    if off:
        after = flat_ref[row + 1 : row + 17, :]
        here = jnp.where(
            lane < 128 - off, pltpu.roll(here, 128 - off, axis=1), pltpu.roll(after, 128 - off, axis=1)
        )
    return here


def step_kernel(
    zb_ref, zh_ref, column_ref, own_ref, other_ref, current_ref, update_ref, out_ref, moment_ref
):
    zb, zh = zb_ref[0], zh_ref[0]
    moment_ref[zb] = own_ref[...]
    moment_ref[1 - zb] = other_ref[...]
    for b in range(2):
        gradient = column_ref[0, 16 * b : 16 * b + 16, :].astype(F32)
        for i in range(1, 16):
            gradient = gradient + column_ref[i, 16 * b : 16 * b + 16, :].astype(F32)
        gradient = gradient * (1.0 / 393216)
        current = current_ref[b]
        first = 0.9 * moment_ref[b, 0] + 0.1 * gradient
        second = 0.95 * moment_ref[b, 1] + 0.05 * gradient * gradient
        update = first / (1.0 - 0.9**STEP) / (jnp.sqrt(second / (1.0 - 0.95**STEP)) + 1e-08)
        stepped = (current - 0.005 * (update + 0.1 * current)).astype(BF16)
        moment_ref[b, 0] = update
        for i in range(16):
            out_ref[i, 16 * b : 16 * b + 16, :] = stepped
    update_ref[...] = moment_ref[zb, 0]
    for slot in range(12):
        tile = column_ref[4 * (zh ^ (slot // 4 + 1)) + slot % 4, 32:48, :]
        for i in range(16):
            out_ref[i, 32 + 16 * slot : 48 + 16 * slot, :] = tile


def stepped_kernel(spread_ref, out_ref):
    out_ref[...] = spread_ref[:, 0:32, :]


def rows_kernel(za_ref, own_ref, other_ref, out_ref, pair_ref, flat_ref, rows_ref):
    za = za_ref[0]
    pair_ref[za] = own_ref[...]
    pair_ref[1 - za] = other_ref[...]
    for p in range(16):
        lay(
            flat_ref.at[p],
            [pair_ref[q % 2, p, 16 * (q // 2) : 16 * (q // 2) + 16, :].astype(F32) for q in range(4)],
        )
        for k in range(9):
            rows_ref[7 * p : 7 * p + 7, 128 * k : 128 * k + 128] = flat_ref[p, pl.ds(k, 7, stride=9), :]
    out_ref[...] = rows_ref[...].astype(BF16)


def input_kernel(core_ref, zh_ref, c_ref, mine_ref, yours_ref, own_ref, other_ref, out_ref, whole_ref, part_ref, sem):
    core, zh = core_ref[0], zh_ref[0]
    for rows_ref, ref, half in ((mine_ref, own_ref, core), (yours_ref, other_ref, 1 - core)):
        whole_ref[pl.ds(pl.multiple_of(224 * zh + 112 * half, 16), 112), :] = rows_ref[...]
        for d in (1, 2, 3):
            for t in range(63):
                low = pl.multiple_of(224 * (zh ^ d) + 112 * half + 16 * (t // 9), 16)
                slot = 32 + 16 * (4 * (d - 1) + t % 4)
                whole_ref[pl.ds(low, 16), 128 * (t % 9) : 128 * (t % 9) + 128] = ref[
                    t // 4, slot : slot + 16, :
                ]
    copies = []
    for i in range(3):
        part_ref[i] = lax.dot_general(
            c_ref[256 * i : 256 * i + 256, :],
            whole_ref[...],
            (((1,), (1,)), ((), ())),
            preferred_element_type=F32,
        ).astype(BF16)
        copies.append(pltpu.make_async_copy(part_ref.at[i], out_ref.at[pl.ds(256 * i, 256)], sem.at[i]))
        copies[-1].start()
    for copy in copies:
        copy.wait()


def call(kernel, outs, operands, specs, scratch=(), out_spec=VMEM):
    return pl.pallas_call(
        kernel,
        out_shape=outs,
        in_specs=specs,
        out_specs=jax.tree.map(lambda _: out_spec, outs),
        scratch_shapes=list(scratch),
        compiler_params=PARAMS,
    )(*operands)


def shards(inputs, cotangent, weight, moment_one, moment_two):
    shape = jax.ShapeDtypeStruct
    core = lax.axis_index("core").astype(jnp.int32).reshape(1)
    za, zb, zh = (lax.axis_index(a).astype(jnp.int32).reshape(1) for a in ("za", "zb", "zh"))
    own = lax.axis_index(("y", "x", "zb", "za"))

    turned = call(turn_kernel, shape((2, 2, 256, 768), BF16), (inputs,), [VMEM])

    def term(half):
        return call(term_kernel, shape((16, 32, 1152), BF16), (half, turned, cotangent), [SMEM, VMEM, VMEM])

    send = term(1 - core)
    got = lax.ppermute(send, "core", [(0, 1), (1, 0)])
    kept = term(core)
    chip = call(add_kernel, shape((16, 32, 1152), BF16), (kept, got), [VMEM, VMEM])
    own_tile = jnp.minimum(own, 62)
    tile = lax.dynamic_slice(weight, (16 * (own_tile // 9), 128 * (own_tile % 9)), (16, 128))
    flat = weight.reshape(-1)
    pair = own // 4 * 4 + lax.axis_index("za")
    current = [lax.dynamic_slice_in_dim(flat, (pair + 2 * b) * 2016, 2016, 0).astype(F32) for b in range(2)]
    current = jnp.stack([jnp.pad(a, (0, 32)).reshape(16, 128) for a in current])
    moments = jnp.stack([jnp.pad(a, (0, 32)).reshape(16, 128) for a in (moment_one, moment_two)])
    moments, mine, chip = lax.optimization_barrier((moments, weight, chip))
    plane = lax.all_to_all(chip, ("y", "x"), 0, 0)
    near = lax.ppermute(moments, "zb", [(0, 1), (1, 0)])
    yours = lax.ppermute(mine, "core", [(0, 1), (1, 0)])
    plane, yours, near = lax.optimization_barrier((plane, yours, near))
    column = call(
        column_kernel,
        shape((16, 48, 128), BF16),
        (plane, tile),
        [VMEM, VMEM],
        [pltpu.VMEM((4, 72, 128), F32)],
    )
    column = lax.all_to_all(column, ("zh", "zb", "za"), 0, 0)
    update, spread = call(
        step_kernel,
        (shape((16, 128), F32), shape((16, 224, 128), BF16)),
        (zb, zh, column, moments, near, current),
        [SMEM] * 2 + [VMEM] * 4,
        [pltpu.VMEM((2, 2, 16, 128), F32)],
    )
    spread = lax.all_to_all(spread, ("y", "x"), 0, 0)
    others = lax.ppermute(spread, "core", [(0, 1), (1, 0)])
    half = call(stepped_kernel, shape((16, 32, 128), BF16), (spread,), [VMEM])
    other = lax.ppermute(half, "za", [(0, 1), (1, 0)])
    grad_in = call(
        input_kernel,
        shape((768, 896), BF16),
        (core, zh, cotangent, weight, yours, spread, others),
        [SMEM] * 2 + [VMEM] * 5,
        [
            pltpu.VMEM((896, 1152), BF16),
            pltpu.VMEM((3, 256, 896), BF16),
            pltpu.SemaphoreType.DMA((3,)),
        ],
        pl.BlockSpec(memory_space=pl.ANY),
    )
    half, other, grad_in = lax.optimization_barrier((half, other, grad_in))
    new_weight = call(
        rows_kernel,
        shape((112, 1152), BF16),
        (za, half, other),
        [SMEM, VMEM, VMEM],
        [pltpu.VMEM((2, 16, 32, 128), BF16), pltpu.VMEM((16, 72, 128), F32), pltpu.VMEM((112, 1152), F32)],
    )
    return (grad_in, update.reshape(2048)[:2016], new_weight)


def solution(mesh):
    fine = Mesh(mesh.devices.reshape(SIZES), AXES)
    return jax.shard_map(
        shards,
        mesh=fine,
        in_specs=(
            P(AXES, None),
            P(AXES, None),
            P(("zh", "core"), None),
            P(AXES),
            P(AXES),
        ),
        out_specs=(P(AXES, None), P(AXES), P(("zh", "core"), None)),
        check_vma=False,
    )
```

time: 104 us -> 101 us (0.971)
  the two profiles are of different devices: /device:TPU:33 before, /device:TPU:1 now
where the time goes in v4:
time: 101 us
  starting transfers between devices  43.2 us (43%)
  waiting for transfers between devices  27.6 us (27%)
  blocking collectives  16 us (16%)
  Pallas kernels  10.6 us (10%)
  local copies, waits for them, and re-layouts  2.2 us (2%)
    all_to_all x1, blocking collectives, shards(): spread = lax.all_to_all(spread, ('y', 'x'), 0, 0)  16 us
    all_to_all x1, waiting for transfers between devices, shards(): column = lax.all_to_all(column, ('zh', 'zb', 'za'), 0, 0)  11.9 us
    all_to_all x1, starting transfers between devices, shards(): column = lax.all_to_all(column, ('zh', 'zb', 'za'), 0, 0)  11.3 us
    all_to_all x1, waiting for transfers between devices, shards(): plane = lax.all_to_all(chip, ('y', 'x'), 0, 0)  11 us
    pallas_call x9, Pallas kernels, call(): pl.pallas_call(kernel, out_shape=outs, in_specs=specs, out_specs=jax.tree...  10.6 us
    ppermute x1, starting transfers between devices, shards(): got = lax.ppermute(send, 'core', [(0, 1), (1, 0)])  8.79 us
    ppermute x1, starting transfers between devices, shards(): others = lax.ppermute(spread, 'core', [(0, 1), (1, 0)])  7.86 us
    ppermute x1, starting transfers between devices, shards(): other = lax.ppermute(half, 'za', [(0, 1), (1, 0)])  6.28 us
  transfers between devices with their start and end apart: 7, of which 5 were waited for; matrix products, arithmetic and copies ran while one was open for 0% of the time, Pallas kernels for 5%

profile of v4, /device:TPU:1, one launch (start us, length us, event | category | flops | bytes accessed | tf_op | source)
XLA Modules:
  0.0 100.5 jit_solution(16002175180038998411)
XLA Ops:
  0.6 1.3 %copy-done.1 = bf16[768,896]{1,0:T(8,128)(2,1)S(1)} copy-done((bf16[768,896]{1,0:T(8,128)(2,1)S(1)}, bf16[768,896]{1,0:T(8,128)(2,1)}, u32[]{:S(2)}) %copy-start.1) | copy-done | bytes 1376280
  2.0 1.0 %shard_map.76.turned_ref = bf16[2,2,256,768]{3,2,1,0:T(8,128)(2,1)S(1)} custom-call(bf16[768,896]{1,0:T(8,128)(2,1)S(1)} %copy-done.1), custom_call_target="tpu_custom_call" | custom-call | tf_op jit(solution)/shard_map/pallas_call | solution.py:154
  3.0 0.4 copy-done
  3.5 1.2 %shard_map.78 = bf16[16,32,1152]{2,1,0:T(8,128)(2,1)S(1)} custom-call(s32[1]{0:T(128)S(6)} %sub.10.half_ref, bf16[2,2,256,768]{3,2,1,0:T(8,128)(2,1)S(1)} %shard_map.76.turned_ref, bf16[768,1152]{1,0:T(8,128)(2,1)S(1)} %copy-done), custom_call_target="tpu_custom_call" | custom-call | tf_op jit(solution)/shard_map/pallas_call | solution.py:154
  4.7 8.8 %collective-permute-start = (bf16[16,32,1152]{2,1,0:T(8,128)(2,1)S(1)}, bf16[16,32,1152]{2,1,0:T(8,128)(2,1)S(1)}, u32[]{:S(2)}, u32[]{:S(2)}) collective-permute-start(bf16[16,32,1152]{2,1,0:T(8,128)(2,1)S(1)} %shard_map.78), channel_id=1, source_target_pairs={{0,64},{64,0},{1,65},{65,1},{2,66},{66,2},{3,67},{67,3},{4,68},{68... | collective-permute-start | bytes 3538952 | tf_op jit(solution)/shard_map/ppermute | solution.py:176
  13.5 1.2 %shard_map.77.kept_ref = bf16[16,32,1152]{2,1,0:T(8,128)(2,1)S(1)} custom-call(s32[1]{0:T(128)} %bitcast.4.half_ref.core_ref, bf16[2,2,256,768]{3,2,1,0:T(8,128)(2,1)S(1)} %shard_map.76.turned_ref, bf16[768,1152]{1,0:T(8,128)(2,1)S(1)} %copy-done), custom_call_target="tpu_custom_call" | custom-call | tf_op jit(solution)/shard_map/pallas_call | solution.py:154
  14.7 1.2 %collective-permute-done.got_ref = bf16[16,32,1152]{2,1,0:T(8,128)(2,1)S(1)} collective-permute-done((bf16[16,32,1152]{2,1,0:T(8,128)(2,1)S(1)}, bf16[16,32,1152]{2,1,0:T(8,128)(2,1)S(1)}, u32[]{:S(2)}, u32[]{:S(2)}) %collective-permute-start) | collective-permute-done | bytes 1179680 | tf_op jit(solution)/shard_map/ppermute | solution.py:176
  15.9 1.2 %shard_map.79 = bf16[16,32,1152]{2,1,0:T(8,128)(2,1)} custom-call(bf16[16,32,1152]{2,1,0:T(8,128)(2,1)S(1)} %shard_map.77.kept_ref, bf16[16,32,1152]{2,1,0:T(8,128)(2,1)S(1)} %collective-permute-done.got_ref), custom_call_target="tpu_custom_call" | custom-call | tf_op jit(solution)/shard_map/pallas_call | solution.py:154
  17.1 3.8 %all-to-all-start = ((bf16[16,32,1152]{2,1,0:T(8,128)(2,1)}), bf16[16,32,1152]{2,1,0:T(8,128)(2,1)S(1)}, u32[]{:S(2)}, u32[]{:S(2)}) async-start(bf16[16,32,1152]{2,1,0:T(8,128)(2,1)} %shard_map.79), calls=%async_computation | async-start | bytes 2359296 | tf_op jit(solution)/shard_map/all_to_all | solution.py:187
  21.0 2.3 %collective-permute-start.1 = (bf16[112,1152]{1,0:T(8,128)(2,1)S(1)}, bf16[112,1152]{1,0:T(8,128)(2,1)S(1)}, u32[]{:S(2)}, u32[]{:S(2)}) collective-permute-start(bf16[112,1152]{1,0:T(8,128)(2,1)S(1)} %copy-done.2), channel_id=1, source_target_pairs={{0,64},{64,0},{1,65},{65,1},{2,66},{66,2},{3,67},{67,3},{4,68},{68... | collective-permute-start | bytes 774152 | tf_op jit(solution)/shard_map/ppermute | solution.py:189
  23.3 2.9 %collective-permute-start.2 = (f32[2,16,128]{2,1,0:T(8,128)S(1)}, f32[2,16,128]{2,1,0:T(8,128)S(1)}, u32[]{:S(2)}, u32[]{:S(2)}) collective-permute-start(f32[2,16,128]{2,1,0:T(8,128)S(1)} %pad_maximum_fusion.own_ref), channel_id=1, source_target_pairs={{0,2},{2,0},{1,3},{3,1},{4,6},{6,4},{5,7},{7,5},{8,10},{10,8},{9,1... | collective-permute-start | bytes 49160 | tf_op jit(solution)/shard_map/ppermute | solution.py:188
  26.2 3.0 %collective-permute-done.2.other_ref = f32[2,16,128]{2,1,0:T(8,128)S(1)} collective-permute-done((f32[2,16,128]{2,1,0:T(8,128)S(1)}, f32[2,16,128]{2,1,0:T(8,128)S(1)}, u32[]{:S(2)}, u32[]{:S(2)}) %collective-permute-start.2) | collective-permute-done | bytes 16416 | tf_op jit(solution)/shard_map/ppermute | solution.py:188
  29.3 11.0 %all-to-all-done.plane_ref = bf16[16,32,1152]{2,1,0:T(8,128)(2,1)S(1)} async-done(((bf16[16,32,1152]{2,1,0:T(8,128)(2,1)}), bf16[16,32,1152]{2,1,0:T(8,128)(2,1)S(1)}, u32[]{:S(2)}, u32[]{:S(2)}) %all-to-all-start) | async-done | bytes 1179680 | tf_op jit(solution)/shard_map/all_to_all | solution.py:187
  40.2 0.9 shard_map.80
  41.1 11.3 %all-to-all-start.1 = ((bf16[16,48,128]{2,1,0:T(8,128)(2,1)}), bf16[16,48,128]{2,1,0:T(8,128)(2,1)S(1)}, u32[]{:S(2)}, u32[]{:S(2)}) async-start(bf16[16,48,128]{2,1,0:T(8,128)(2,1)} %shard_map.80), calls=%async_computation.1 | async-start | bytes 393216 | tf_op jit(solution)/shard_map/all_to_all | solution.py:198
  52.4 0.3 reshape.27
  52.9 11.9 %all-to-all-done.1.column_ref = bf16[16,48,128]{2,1,0:T(8,128)(2,1)S(1)} async-done(((bf16[16,48,128]{2,1,0:T(8,128)(2,1)}), bf16[16,48,128]{2,1,0:T(8,128)(2,1)S(1)}, u32[]{:S(2)}, u32[]{:S(2)}) %all-to-all-start.1) | async-done | bytes 196640 | tf_op jit(solution)/shard_map/all_to_all | solution.py:198
  64.8 0.7 shard_map.81
  65.5 16.0 %all_to_all.15.spread_ref.own_ref = bf16[16,224,128]{2,1,0:T(8,128)(2,1)S(1)} all-to-all(bf16[16,224,128]{2,1,0:T(8,128)(2,1)S(1)} %get-tuple-element.19), channel_id=1, replica_groups=mesh['zh'=4,'core'=2,'y'=4,'x'=4,'zb'=2,'za'=2] {'y','x'}, dimensions={0} | all-to-all | bytes 1835008 | tf_op jit(solution)/shard_map/all_to_all | solution.py:206
  81.6 7.9 %collective-permute-start.4 = (bf16[16,224,128]{2,1,0:T(8,128)(2,1)S(1)}, bf16[16,224,128]{2,1,0:T(8,128)(2,1)S(1)}, u32[]{:S(2)}, u32[]{:S(2)}) collective-permute-start(bf16[16,224,128]{2,1,0:T(8,128)(2,1)S(1)} %all_to_all.15.spread_ref.own_ref), channel_id=1, source_target_pairs={{0,64},{64,0},{1,65},{65,1},{2,66},{66,2},{3,67},{67,3},{4,68},{68... | collective-permute-start | bytes 2752520 | tf_op jit(solution)/shard_map/ppermute | solution.py:207
  89.5 6.3 %collective-permute-start.3 = (bf16[16,32,128]{2,1,0:T(8,128)(2,1)S(1)}, bf16[16,32,128]{2,1,0:T(8,128)(2,1)S(1)}, u32[]{:S(2)}, u32[]{:S(2)}) collective-permute-start(bf16[16,32,128]{2,1,0:T(8,128)(2,1)S(1)} %shard_map.82.own_ref), channel_id=1, source_target_pairs={{0,1},{1,0},{2,3},{3,2},{4,5},{5,4},{6,7},{7,6},{8,9},{9,8},{10,11... | collective-permute-start | bytes 393224 | tf_op jit(solution)/shard_map/ppermute | solution.py:209
  95.8 3.3 %shard_map.83 = bf16[768,896]{1,0:T(8,128)(2,1)} custom-call(s32[1]{0:T(128)} %bitcast.4.half_ref.core_ref, s32[1]{0:T(128)} %bitcast.1.zh_ref, bf16[768,1152]{1,0:T(8,128)(2,1)S(1)} %copy-done, bf16[112,1152]{1,0:T(8,128)(2,1)S(1)} %copy-done.2, bf16[112,1152]{1,0:T(8,128)(2,1)S(1)} %collective-permute-done.1.yours_ref, ...), custom_call_target="tpu_custom_call" | custom-call | tf_op jit(solution)/shard_map/pallas_call | solution.py:154
  99.1 0.5 collective-permute-done.3.other_ref
  99.6 1.0 shard_map.84
  (17 shorter events, 0.2 us)
Async XLA Ops:
  0.6 1.3 %copy-start.1 = (bf16[768,896]{1,0:T(8,128)(2,1)S(1)}, bf16[768,896]{1,0:T(8,128)(2,1)}, u32[]{:S(2)}) copy-start(bf16[768,896]{1,0:T(8,128)(2,1)} %x_ref.1) | copy-start | bytes 4128772
  2.0 1.5 %copy-start = (bf16[768,1152]{1,0:T(8,128)(2,1)S(1)}, bf16[768,1152]{1,0:T(8,128)(2,1)}, u32[]{:S(2)}) copy-start(bf16[768,1152]{1,0:T(8,128)(2,1)} %c_ref.5) | copy-start | bytes 5308420
  4.7 10.0 %copy-start.3 = (f32[2016]{0:T(1024)S(1)}, f32[2016]{0:T(1024)}, u32[]{:S(2)}) copy-start(f32[2016]{0:T(1024)} %param.9) | copy-start | bytes 24196
  4.7 10.0 %copy-start.4 = (f32[2016]{0:T(1024)S(1)}, f32[2016]{0:T(1024)}, u32[]{:S(2)}) copy-start(f32[2016]{0:T(1024)} %param.8) | copy-start | bytes 24196
  4.7 11.2 %collective-permute-start = (bf16[16,32,1152]{2,1,0:T(8,128)(2,1)S(1)}, bf16[16,32,1152]{2,1,0:T(8,128)(2,1)S(1)}, u32[]{:S(2)}, u32[]{:S(2)}) collective-permute-start(bf16[16,32,1152]{2,1,0:T(8,128)(2,1)S(1)} %shard_map.78), channel_id=1, source_target_pairs={{0,64},{64,0},{1,65},{65,1},{2,66},{66,2},{3,67},{67,3},{4,68},{68... | collective-permute-start | bytes 3538952 | tf_op jit(solution)/shard_map/ppermute | solution.py:176
  17.1 3.8 %copy-start.2 = (bf16[112,1152]{1,0:T(8,128)(2,1)S(1)}, bf16[112,1152]{1,0:T(8,128)(2,1)}, u32[]{:S(2)}) copy-start(bf16[112,1152]{1,0:T(8,128)(2,1)} %mine_ref.1) | copy-start | bytes 774148
  17.1 23.1 %all-to-all-start = ((bf16[16,32,1152]{2,1,0:T(8,128)(2,1)}), bf16[16,32,1152]{2,1,0:T(8,128)(2,1)S(1)}, u32[]{:S(2)}, u32[]{:S(2)}) async-start(bf16[16,32,1152]{2,1,0:T(8,128)(2,1)} %shard_map.79), calls=%async_computation | async-start | bytes 2359296 | tf_op jit(solution)/shard_map/all_to_all | solution.py:187
  21.0 8.3 %collective-permute-start.1 = (bf16[112,1152]{1,0:T(8,128)(2,1)S(1)}, bf16[112,1152]{1,0:T(8,128)(2,1)S(1)}, u32[]{:S(2)}, u32[]{:S(2)}) collective-permute-start(bf16[112,1152]{1,0:T(8,128)(2,1)S(1)} %copy-done.2), channel_id=1, source_target_pairs={{0,64},{64,0},{1,65},{65,1},{2,66},{66,2},{3,67},{67,3},{4,68},{68... | collective-permute-start | bytes 774152 | tf_op jit(solution)/shard_map/ppermute | solution.py:189
  23.3 6.0 %collective-permute-start.2 = (f32[2,16,128]{2,1,0:T(8,128)S(1)}, f32[2,16,128]{2,1,0:T(8,128)S(1)}, u32[]{:S(2)}, u32[]{:S(2)}) collective-permute-start(f32[2,16,128]{2,1,0:T(8,128)S(1)} %pad_maximum_fusion.own_ref), channel_id=1, source_target_pairs={{0,2},{2,0},{1,3},{3,1},{4,6},{6,4},{5,7},{7,5},{8,10},{10,8},{9,1... | collective-permute-start | bytes 49160 | tf_op jit(solution)/shard_map/ppermute | solution.py:188
  41.1 23.6 %all-to-all-start.1 = ((bf16[16,48,128]{2,1,0:T(8,128)(2,1)}), bf16[16,48,128]{2,1,0:T(8,128)(2,1)S(1)}, u32[]{:S(2)}, u32[]{:S(2)}) async-start(bf16[16,48,128]{2,1,0:T(8,128)(2,1)} %shard_map.80), calls=%async_computation.1 | async-start | bytes 393216 | tf_op jit(solution)/shard_map/all_to_all | solution.py:198
  81.6 14.2 %collective-permute-start.4 = (bf16[16,224,128]{2,1,0:T(8,128)(2,1)S(1)}, bf16[16,224,128]{2,1,0:T(8,128)(2,1)S(1)}, u32[]{:S(2)}, u32[]{:S(2)}) collective-permute-start(bf16[16,224,128]{2,1,0:T(8,128)(2,1)S(1)} %all_to_all.15.spread_ref.own_ref), channel_id=1, source_target_pairs={{0,64},{64,0},{1,65},{65,1},{2,66},{66,2},{3,67},{67,3},{4,68},{68... | collective-permute-start | bytes 2752520 | tf_op jit(solution)/shard_map/ppermute | solution.py:207
  89.5 10.1 %collective-permute-start.3 = (bf16[16,32,128]{2,1,0:T(8,128)(2,1)S(1)}, bf16[16,32,128]{2,1,0:T(8,128)(2,1)S(1)}, u32[]{:S(2)}, u32[]{:S(2)}) collective-permute-start(bf16[16,32,128]{2,1,0:T(8,128)(2,1)S(1)} %shard_map.82.own_ref), channel_id=1, source_target_pairs={{0,1},{1,0},{2,3},{3,2},{4,5},{5,4},{6,7},{7,6},{8,9},{9,8},{10,11... | collective-permute-start | bytes 393224 | tf_op jit(solution)/shard_map/ppermute | solution.py:209

commit v5 on v4

--- a/solution.py
+++ b/solution.py
@@ -1,5 +1,6 @@
 import jax
 import jax.numpy as jnp
+import numpy as np
 from jax import lax
 from jax.experimental import pallas as pl
 from jax.experimental.pallas import tpu as pltpu
@@ -8,6 +9,7 @@
 STEP = 10
 AXES = ("zh", "core", "y", "x", "zb", "za")
 SIZES = (4, 2, 4, 4, 2, 2)
+PLANE, COLUMN = 10, 2
 BF16, F32 = jnp.bfloat16, jnp.float32
 VMEM = pl.BlockSpec(memory_space=pltpu.VMEM)
 SMEM = pl.BlockSpec(memory_space=pltpu.SMEM)
@@ -21,7 +23,7 @@
             place = lax.broadcasted_iota(jnp.int32, (256, 512), 0)
             column = lax.broadcasted_iota(jnp.int32, (256, 512), 1)
             row = place & 7
-            source = (2 * pair + ((place >> 3) & 1)) * 224 + half * 112 + (place >> 4) * 7 + row - low
+            source = (2 * pair + ((place >> 3) & 1)) * 224 + half * 112 + ((place >> 4) ^ PLANE) * 7 + row - low
             pick = jnp.where((source == column) & (row < 7), 1.0, 0.0).astype(BF16)
             out_ref[half, pair] = lax.dot_general(
                 pick, x_ref[:, low : low + 512], (((1,), (1,)), ((), ())), preferred_element_type=F32
@@ -49,9 +51,9 @@
             flat_ref[zh, pl.ds(k, 8, stride=9), :] = total[8 * zh : 8 * zh + 8, 128 * k : 128 * k + 128]
         quarters = [cut(flat_ref.at[zh], q).astype(BF16) for q in range(4)]
         for zl in range(4):
-            out_ref[4 * zh + zl, 0:16, :] = quarters[zl % 2]
-            out_ref[4 * zh + zl, 16:32, :] = quarters[zl % 2 + 2]
-            out_ref[4 * zh + zl, 32:48, :] = tile
+            out_ref[4 * (zh ^ COLUMN) + zl, 0:16, :] = quarters[zl % 2]
+            out_ref[4 * (zh ^ COLUMN) + zl, 16:32, :] = quarters[zl % 2 + 2]
+            out_ref[4 * (zh ^ COLUMN) + zl, 32:48, :] = tile
 
 
 def lay(flat_ref, pieces):
@@ -102,7 +104,7 @@
             out_ref[i, 16 * b : 16 * b + 16, :] = stepped
     update_ref[...] = moment_ref[zb, 0]
     for slot in range(12):
-        tile = column_ref[4 * (zh ^ (slot // 4 + 1)) + slot % 4, 32:48, :]
+        tile = column_ref[4 * (zh ^ (slot // 4 + 1) ^ COLUMN) + slot % 4, 32:48, :]
         for i in range(16):
             out_ref[i, 32 + 16 * slot : 48 + 16 * slot, :] = tile
 
@@ -121,7 +123,7 @@
             [pair_ref[q % 2, p, 16 * (q // 2) : 16 * (q // 2) + 16, :].astype(F32) for q in range(4)],
         )
         for k in range(9):
-            rows_ref[7 * p : 7 * p + 7, 128 * k : 128 * k + 128] = flat_ref[p, pl.ds(k, 7, stride=9), :]
+            rows_ref[7 * (p ^ PLANE) : 7 * (p ^ PLANE) + 7, 128 * k : 128 * k + 128] = flat_ref[p, pl.ds(k, 7, stride=9), :]
     out_ref[...] = rows_ref[...].astype(BF16)
 
 
@@ -134,7 +136,7 @@
                 low = pl.multiple_of(224 * (zh ^ d) + 112 * half + 16 * (t // 9), 16)
                 slot = 32 + 16 * (4 * (d - 1) + t % 4)
                 whole_ref[pl.ds(low, 16), 128 * (t % 9) : 128 * (t % 9) + 128] = ref[
-                    t // 4, slot : slot + 16, :
+                    (t // 4) ^ PLANE, slot : slot + 16, :
                 ]
     copies = []
     for i in range(3):
@@ -161,6 +163,15 @@
     )(*operands)
 
 
+def exchange(a, over):
+    ids = np.arange(512).reshape(4, 2, 16, 4)
+    if over == "plane":
+        groups = ids[:, :, np.arange(16) ^ PLANE].transpose(0, 1, 3, 2).reshape(32, 16)
+    else:
+        groups = ids[np.arange(4) ^ COLUMN].transpose(1, 2, 0, 3).reshape(32, 16)
+    return lax.all_to_all(a, AXES, 0, 0, axis_index_groups=groups.tolist())
+
+
 def shards(inputs, cotangent, weight, moment_one, moment_two):
     shape = jax.ShapeDtypeStruct
     core = lax.axis_index("core").astype(jnp.int32).reshape(1)
@@ -184,7 +195,7 @@
     current = jnp.stack([jnp.pad(a, (0, 32)).reshape(16, 128) for a in current])
     moments = jnp.stack([jnp.pad(a, (0, 32)).reshape(16, 128) for a in (moment_one, moment_two)])
     moments, mine, chip = lax.optimization_barrier((moments, weight, chip))
-    plane = lax.all_to_all(chip, ("y", "x"), 0, 0)
+    plane = exchange(chip, "plane")
     near = lax.ppermute(moments, "zb", [(0, 1), (1, 0)])
     yours = lax.ppermute(mine, "core", [(0, 1), (1, 0)])
     plane, yours, near = lax.optimization_barrier((plane, yours, near))
@@ -195,7 +206,7 @@
         [VMEM, VMEM],
         [pltpu.VMEM((4, 72, 128), F32)],
     )
-    column = lax.all_to_all(column, ("zh", "zb", "za"), 0, 0)
+    column = exchange(column, "column")
     update, spread = call(
         step_kernel,
         (shape((16, 128), F32), shape((16, 224, 128), BF16)),
@@ -203,7 +214,7 @@
         [SMEM] * 2 + [VMEM] * 4,
         [pltpu.VMEM((2, 2, 16, 128), F32)],
     )
-    spread = lax.all_to_all(spread, ("y", "x"), 0, 0)
+    spread = exchange(spread, "plane")
     others = lax.ppermute(spread, "core", [(0, 1), (1, 0)])
     half = call(stepped_kernel, shape((16, 32, 128), BF16), (spread,), [VMEM])
     other = lax.ppermute(half, "za", [(0, 1), (1, 0)])

time: 101 us -> 93.6 us (0.927)
  waiting for transfers between devices: 27.6 us -> 19.5 us
  blocking collectives: 16 us -> 19 us
  starting transfers between devices: 43.2 us -> 40.8 us
    all_to_all x2, waiting for transfers between devices: 22.9 us -> 13.5 us  [exchange(): return lax.all_to_all(a, AXES, 0, 0, axis_index_groups=groups.tolist())]
    all_to_all x2, starting transfers between devices: 15.1 us -> 22 us  [exchange(): return lax.all_to_all(a, AXES, 0, 0, axis_index_groups=groups.tolist())]
    ppermute x1, starting transfers between devices: 7.86 us -> 2.71 us  [shards(): others = lax.ppermute(spread, 'core', [(0, 1), (1, 0)])]
    ppermute x1, starting transfers between devices: 6.28 us -> 2.59 us  [shards(): other = lax.ppermute(half, 'za', [(0, 1), (1, 0)])]
    all_to_all x1, blocking collectives: 16 us -> 19 us  [exchange(): return lax.all_to_all(a, AXES, 0, 0, axis_index_groups=groups.tolist())]
where the time goes in v5:
time: 93.6 us; the launch traced here: 93 us
  starting transfers between devices  40.8 us (44%)
  waiting for transfers between devices  19.5 us (21%)
  blocking collectives  19 us (20%)
  Pallas kernels  10.6 us (11%)
  local copies, waits for them, and re-layouts  2.16 us (2%)
    all_to_all x2, starting transfers between devices, exchange(): return lax.all_to_all(a, AXES, 0, 0, axis_index_groups=groups.tolist())  22 us
    all_to_all x1, blocking collectives, exchange(): return lax.all_to_all(a, AXES, 0, 0, axis_index_groups=groups.tolist())  19 us
    all_to_all x2, waiting for transfers between devices, exchange(): return lax.all_to_all(a, AXES, 0, 0, axis_index_groups=groups.tolist())  13.5 us
    pallas_call x9, Pallas kernels, call(): pl.pallas_call(kernel, out_shape=outs, in_specs=specs, out_specs=jax.tree...  10.6 us
    ppermute x1, starting transfers between devices, shards(): got = lax.ppermute(send, 'core', [(0, 1), (1, 0)])  8.79 us
    ppermute x1, waiting for transfers between devices, shards(): near = lax.ppermute(moments, 'zb', [(0, 1), (1, 0)])  3.68 us
    ppermute x1, starting transfers between devices, shards(): yours = lax.ppermute(mine, 'core', [(0, 1), (1, 0)])  2.84 us
    ppermute x1, starting transfers between devices, shards(): others = lax.ppermute(spread, 'core', [(0, 1), (1, 0)])  2.71 us
  transfers between devices with their start and end apart: 7, of which 5 were waited for; matrix products, arithmetic and copies ran while one was open for 0% of the time, Pallas kernels for 5%

profile of v5, /device:TPU:1, one launch (start us, length us, event | category | flops | bytes accessed | tf_op | source)
XLA Modules:
  0.0 93.0 jit_solution(2687224874173388609)
XLA Ops:
  0.6 1.3 %copy-done.1 = bf16[768,896]{1,0:T(8,128)(2,1)S(1)} copy-done((bf16[768,896]{1,0:T(8,128)(2,1)S(1)}, bf16[768,896]{1,0:T(8,128)(2,1)}, u32[]{:S(2)}) %copy-start.1) | copy-done | bytes 1376280
  2.0 1.1 %shard_map.76.turned_ref = bf16[2,2,256,768]{3,2,1,0:T(8,128)(2,1)S(1)} custom-call(bf16[768,896]{1,0:T(8,128)(2,1)S(1)} %copy-done.1), custom_call_target="tpu_custom_call" | custom-call | tf_op jit(solution)/shard_map/pallas_call | solution.py:156
  3.0 0.4 copy-done
  3.5 1.2 %shard_map.78 = bf16[16,32,1152]{2,1,0:T(8,128)(2,1)S(1)} custom-call(s32[1]{0:T(128)S(6)} %sub.10.half_ref, bf16[2,2,256,768]{3,2,1,0:T(8,128)(2,1)S(1)} %shard_map.76.turned_ref, bf16[768,1152]{1,0:T(8,128)(2,1)S(1)} %copy-done), custom_call_target="tpu_custom_call" | custom-call | tf_op jit(solution)/shard_map/pallas_call | solution.py:156
  4.7 8.8 %collective-permute-start = (bf16[16,32,1152]{2,1,0:T(8,128)(2,1)S(1)}, bf16[16,32,1152]{2,1,0:T(8,128)(2,1)S(1)}, u32[]{:S(2)}, u32[]{:S(2)}) collective-permute-start(bf16[16,32,1152]{2,1,0:T(8,128)(2,1)S(1)} %shard_map.78), channel_id=1, source_target_pairs={{0,64},{64,0},{1,65},{65,1},{2,66},{66,2},{3,67},{67,3},{4,68},{68... | collective-permute-start | bytes 3538952 | tf_op jit(solution)/shard_map/ppermute | solution.py:187
  13.5 1.2 %shard_map.77.kept_ref = bf16[16,32,1152]{2,1,0:T(8,128)(2,1)S(1)} custom-call(s32[1]{0:T(128)} %bitcast.4.half_ref.core_ref, bf16[2,2,256,768]{3,2,1,0:T(8,128)(2,1)S(1)} %shard_map.76.turned_ref, bf16[768,1152]{1,0:T(8,128)(2,1)S(1)} %copy-done), custom_call_target="tpu_custom_call" | custom-call | tf_op jit(solution)/shard_map/pallas_call | solution.py:156
  14.7 1.2 %collective-permute-done.got_ref = bf16[16,32,1152]{2,1,0:T(8,128)(2,1)S(1)} collective-permute-done((bf16[16,32,1152]{2,1,0:T(8,128)(2,1)S(1)}, bf16[16,32,1152]{2,1,0:T(8,128)(2,1)S(1)}, u32[]{:S(2)}, u32[]{:S(2)}) %collective-permute-start) | collective-permute-done | bytes 1179680 | tf_op jit(solution)/shard_map/ppermute | solution.py:187
  15.9 1.2 %shard_map.79 = bf16[16,32,1152]{2,1,0:T(8,128)(2,1)} custom-call(bf16[16,32,1152]{2,1,0:T(8,128)(2,1)S(1)} %shard_map.77.kept_ref, bf16[16,32,1152]{2,1,0:T(8,128)(2,1)S(1)} %collective-permute-done.got_ref), custom_call_target="tpu_custom_call" | custom-call | tf_op jit(solution)/shard_map/pallas_call | solution.py:156
  17.1 6.8 %all-to-all-start = ((bf16[16,32,1152]{2,1,0:T(8,128)(2,1)}), bf16[16,32,1152]{2,1,0:T(8,128)(2,1)S(1)}, u32[]{:S(2)}, u32[]{:S(2)}) async-start(bf16[16,32,1152]{2,1,0:T(8,128)(2,1)} %shard_map.79), calls=%async_computation | async-start | bytes 2359296 | tf_op jit(solution)/shard_map/all_to_all | solution.py:172
  23.9 2.8 %collective-permute-start.1 = (bf16[112,1152]{1,0:T(8,128)(2,1)S(1)}, bf16[112,1152]{1,0:T(8,128)(2,1)S(1)}, u32[]{:S(2)}, u32[]{:S(2)}) collective-permute-start(bf16[112,1152]{1,0:T(8,128)(2,1)S(1)} %copy-done.2), channel_id=1, source_target_pairs={{0,64},{64,0},{1,65},{65,1},{2,66},{66,2},{3,67},{67,3},{4,68},{68... | collective-permute-start | bytes 774152 | tf_op jit(solution)/shard_map/ppermute | solution.py:200
  26.8 1.9 %collective-permute-start.2 = (f32[2,16,128]{2,1,0:T(8,128)S(1)}, f32[2,16,128]{2,1,0:T(8,128)S(1)}, u32[]{:S(2)}, u32[]{:S(2)}) collective-permute-start(f32[2,16,128]{2,1,0:T(8,128)S(1)} %pad_maximum_fusion.own_ref), channel_id=1, source_target_pairs={{0,2},{2,0},{1,3},{3,1},{4,6},{6,4},{5,7},{7,5},{8,10},{10,8},{9,1... | collective-permute-start | bytes 49160 | tf_op jit(solution)/shard_map/ppermute | solution.py:199
  28.8 3.7 %collective-permute-done.2.other_ref = f32[2,16,128]{2,1,0:T(8,128)S(1)} collective-permute-done((f32[2,16,128]{2,1,0:T(8,128)S(1)}, f32[2,16,128]{2,1,0:T(8,128)S(1)}, u32[]{:S(2)}, u32[]{:S(2)}) %collective-permute-start.2) | collective-permute-done | bytes 16416 | tf_op jit(solution)/shard_map/ppermute | solution.py:199
  32.5 5.7 %all-to-all-done.plane_ref = bf16[16,32,1152]{2,1,0:T(8,128)(2,1)S(1)} async-done(((bf16[16,32,1152]{2,1,0:T(8,128)(2,1)}), bf16[16,32,1152]{2,1,0:T(8,128)(2,1)S(1)}, u32[]{:S(2)}, u32[]{:S(2)}) %all-to-all-start) | async-done | bytes 1179680 | tf_op jit(solution)/shard_map/all_to_all | solution.py:172
  38.2 0.9 shard_map.80
  39.1 15.2 %all-to-all-start.1 = ((bf16[16,48,128]{2,1,0:T(8,128)(2,1)}), bf16[16,48,128]{2,1,0:T(8,128)(2,1)S(1)}, u32[]{:S(2)}, u32[]{:S(2)}) async-start(bf16[16,48,128]{2,1,0:T(8,128)(2,1)} %shard_map.80), calls=%async_computation.1 | async-start | bytes 393216 | tf_op jit(solution)/shard_map/all_to_all | solution.py:172
  54.3 0.3 reshape.27
  54.7 7.8 %all-to-all-done.1.column_ref = bf16[16,48,128]{2,1,0:T(8,128)(2,1)S(1)} async-done(((bf16[16,48,128]{2,1,0:T(8,128)(2,1)}), bf16[16,48,128]{2,1,0:T(8,128)(2,1)S(1)}, u32[]{:S(2)}, u32[]{:S(2)}) %all-to-all-start.1) | async-done | bytes 196640 | tf_op jit(solution)/shard_map/all_to_all | solution.py:172
  62.6 0.7 shard_map.81
  63.3 19.0 %all_to_all.15.spread_ref.own_ref = bf16[16,224,128]{2,1,0:T(8,128)(2,1)S(1)} all-to-all(bf16[16,224,128]{2,1,0:T(8,128)(2,1)S(1)} %get-tuple-element.19), channel_id=1, replica_groups={{40,44,32,36,56,60,48,52,8,12,0,4,24,28,16,20},{41,45,33,37,57,61,49,53..., dimensions={0} | all-to-all | bytes 1835008 | tf_op jit(solution)/shard_map/all_to_all | solution.py:172
  82.3 2.7 %collective-permute-start.4 = (bf16[16,224,128]{2,1,0:T(8,128)(2,1)S(1)}, bf16[16,224,128]{2,1,0:T(8,128)(2,1)S(1)}, u32[]{:S(2)}, u32[]{:S(2)}) collective-permute-start(bf16[16,224,128]{2,1,0:T(8,128)(2,1)S(1)} %all_to_all.15.spread_ref.own_ref), channel_id=1, source_target_pairs={{0,64},{64,0},{1,65},{65,1},{2,66},{66,2},{3,67},{67,3},{4,68},{68... | collective-permute-start | bytes 2752520 | tf_op jit(solution)/shard_map/ppermute | solution.py:218
  85.0 2.6 %collective-permute-start.3 = (bf16[16,32,128]{2,1,0:T(8,128)(2,1)S(1)}, bf16[16,32,128]{2,1,0:T(8,128)(2,1)S(1)}, u32[]{:S(2)}, u32[]{:S(2)}) collective-permute-start(bf16[16,32,128]{2,1,0:T(8,128)(2,1)S(1)} %shard_map.82.own_ref), channel_id=1, source_target_pairs={{0,1},{1,0},{2,3},{3,2},{4,5},{5,4},{6,7},{7,6},{8,9},{9,8},{10,11... | collective-permute-start | bytes 393224 | tf_op jit(solution)/shard_map/ppermute | solution.py:220
  87.7 3.3 %shard_map.83 = bf16[768,896]{1,0:T(8,128)(2,1)} custom-call(s32[1]{0:T(128)} %bitcast.4.half_ref.core_ref, s32[1]{0:T(128)} %bitcast.1.zh_ref, bf16[768,1152]{1,0:T(8,128)(2,1)S(1)} %copy-done, bf16[112,1152]{1,0:T(8,128)(2,1)S(1)} %copy-done.2, bf16[112,1152]{1,0:T(8,128)(2,1)S(1)} %collective-permute-done.1.yours_ref, ...), custom_call_target="tpu_custom_call" | custom-call | tf_op jit(solution)/shard_map/pallas_call | solution.py:156
  91.0 1.1 %collective-permute-done.3.other_ref = bf16[16,32,128]{2,1,0:T(8,128)(2,1)S(1)} collective-permute-done((bf16[16,32,128]{2,1,0:T(8,128)(2,1)S(1)}, bf16[16,32,128]{2,1,0:T(8,128)(2,1)S(1)}, u32[]{:S(2)}, u32[]{:S(2)}) %collective-permute-start.3) | collective-permute-done | bytes 131104 | tf_op jit(solution)/shard_map/ppermute | solution.py:220
  92.1 1.0 %shard_map.84 = bf16[112,1152]{1,0:T(8,128)(2,1)} custom-call(s32[1]{0:T(128)} %bitcast.8.za_ref, bf16[16,32,128]{2,1,0:T(8,128)(2,1)S(1)} %shard_map.82.own_ref, bf16[16,32,128]{2,1,0:T(8,128)(2,1)S(1)} %collective-permute-done.3.other_ref), custom_call_target="tpu_custom_call" | custom-call | tf_op jit(solution)/shard_map/pallas_call | solution.py:156
  (17 shorter events, 0.2 us)
Async XLA Ops:
  0.6 1.3 %copy-start.1 = (bf16[768,896]{1,0:T(8,128)(2,1)S(1)}, bf16[768,896]{1,0:T(8,128)(2,1)}, u32[]{:S(2)}) copy-start(bf16[768,896]{1,0:T(8,128)(2,1)} %x_ref.1) | copy-start | bytes 4128772
  2.0 1.5 %copy-start = (bf16[768,1152]{1,0:T(8,128)(2,1)S(1)}, bf16[768,1152]{1,0:T(8,128)(2,1)}, u32[]{:S(2)}) copy-start(bf16[768,1152]{1,0:T(8,128)(2,1)} %c_ref.5) | copy-start | bytes 5308420
  4.7 10.0 %copy-start.3 = (f32[2016]{0:T(1024)S(1)}, f32[2016]{0:T(1024)}, u32[]{:S(2)}) copy-start(f32[2016]{0:T(1024)} %param.9) | copy-start | bytes 24196
  4.7 10.0 %copy-start.4 = (f32[2016]{0:T(1024)S(1)}, f32[2016]{0:T(1024)}, u32[]{:S(2)}) copy-start(f32[2016]{0:T(1024)} %param.8) | copy-start | bytes 24196
  4.7 11.2 %collective-permute-start = (bf16[16,32,1152]{2,1,0:T(8,128)(2,1)S(1)}, bf16[16,32,1152]{2,1,0:T(8,128)(2,1)S(1)}, u32[]{:S(2)}, u32[]{:S(2)}) collective-permute-start(bf16[16,32,1152]{2,1,0:T(8,128)(2,1)S(1)} %shard_map.78), channel_id=1, source_target_pairs={{0,64},{64,0},{1,65},{65,1},{2,66},{66,2},{3,67},{67,3},{4,68},{68... | collective-permute-start | bytes 3538952 | tf_op jit(solution)/shard_map/ppermute | solution.py:187
  17.1 6.8 %copy-start.2 = (bf16[112,1152]{1,0:T(8,128)(2,1)S(1)}, bf16[112,1152]{1,0:T(8,128)(2,1)}, u32[]{:S(2)}) copy-start(bf16[112,1152]{1,0:T(8,128)(2,1)} %mine_ref.1) | copy-start | bytes 774148
  17.1 21.1 %all-to-all-start = ((bf16[16,32,1152]{2,1,0:T(8,128)(2,1)}), bf16[16,32,1152]{2,1,0:T(8,128)(2,1)S(1)}, u32[]{:S(2)}, u32[]{:S(2)}) async-start(bf16[16,32,1152]{2,1,0:T(8,128)(2,1)} %shard_map.79), calls=%async_computation | async-start | bytes 2359296 | tf_op jit(solution)/shard_map/all_to_all | solution.py:172
  23.9 8.5 %collective-permute-start.1 = (bf16[112,1152]{1,0:T(8,128)(2,1)S(1)}, bf16[112,1152]{1,0:T(8,128)(2,1)S(1)}, u32[]{:S(2)}, u32[]{:S(2)}) collective-permute-start(bf16[112,1152]{1,0:T(8,128)(2,1)S(1)} %copy-done.2), channel_id=1, source_target_pairs={{0,64},{64,0},{1,65},{65,1},{2,66},{66,2},{3,67},{67,3},{4,68},{68... | collective-permute-start | bytes 774152 | tf_op jit(solution)/shard_map/ppermute | solution.py:200
  26.8 5.7 %collective-permute-start.2 = (f32[2,16,128]{2,1,0:T(8,128)S(1)}, f32[2,16,128]{2,1,0:T(8,128)S(1)}, u32[]{:S(2)}, u32[]{:S(2)}) collective-permute-start(f32[2,16,128]{2,1,0:T(8,128)S(1)} %pad_maximum_fusion.own_ref), channel_id=1, source_target_pairs={{0,2},{2,0},{1,3},{3,1},{4,6},{6,4},{5,7},{7,5},{8,10},{10,8},{9,1... | collective-permute-start | bytes 49160 | tf_op jit(solution)/shard_map/ppermute | solution.py:199
  39.1 23.4 %all-to-all-start.1 = ((bf16[16,48,128]{2,1,0:T(8,128)(2,1)}), bf16[16,48,128]{2,1,0:T(8,128)(2,1)S(1)}, u32[]{:S(2)}, u32[]{:S(2)}) async-start(bf16[16,48,128]{2,1,0:T(8,128)(2,1)} %shard_map.80), calls=%async_computation.1 | async-start | bytes 393216 | tf_op jit(solution)/shard_map/all_to_all | solution.py:172
  82.3 5.3 %collective-permute-start.4 = (bf16[16,224,128]{2,1,0:T(8,128)(2,1)S(1)}, bf16[16,224,128]{2,1,0:T(8,128)(2,1)S(1)}, u32[]{:S(2)}, u32[]{:S(2)}) collective-permute-start(bf16[16,224,128]{2,1,0:T(8,128)(2,1)S(1)} %all_to_all.15.spread_ref.own_ref), channel_id=1, source_target_pairs={{0,64},{64,0},{1,65},{65,1},{2,66},{66,2},{3,67},{67,3},{4,68},{68... | collective-permute-start | bytes 2752520 | tf_op jit(solution)/shard_map/ppermute | solution.py:218
  85.0 7.0 %collective-permute-start.3 = (bf16[16,32,128]{2,1,0:T(8,128)(2,1)S(1)}, bf16[16,32,128]{2,1,0:T(8,128)(2,1)S(1)}, u32[]{:S(2)}, u32[]{:S(2)}) collective-permute-start(bf16[16,32,128]{2,1,0:T(8,128)(2,1)S(1)} %shard_map.82.own_ref), channel_id=1, source_target_pairs={{0,1},{1,0},{2,3},{3,2},{4,5},{5,4},{6,7},{7,6},{8,9},{9,8},{10,11... | collective-permute-start | bytes 393224 | tf_op jit(solution)/shard_map/ppermute | solution.py:220

commit v6 on v5

--- a/solution.py
+++ b/solution.py
@@ -9,7 +9,7 @@
 STEP = 10
 AXES = ("zh", "core", "y", "x", "zb", "za")
 SIZES = (4, 2, 4, 4, 2, 2)
-PLANE, COLUMN = 10, 2
+PLANE, SPREAD, COLUMN = 10, 10, 10
 BF16, F32 = jnp.bfloat16, jnp.float32
 VMEM = pl.BlockSpec(memory_space=pltpu.VMEM)
 SMEM = pl.BlockSpec(memory_space=pltpu.SMEM)
@@ -51,9 +51,9 @@
             flat_ref[zh, pl.ds(k, 8, stride=9), :] = total[8 * zh : 8 * zh + 8, 128 * k : 128 * k + 128]
         quarters = [cut(flat_ref.at[zh], q).astype(BF16) for q in range(4)]
         for zl in range(4):
-            out_ref[4 * (zh ^ COLUMN) + zl, 0:16, :] = quarters[zl % 2]
-            out_ref[4 * (zh ^ COLUMN) + zl, 16:32, :] = quarters[zl % 2 + 2]
-            out_ref[4 * (zh ^ COLUMN) + zl, 32:48, :] = tile
+            out_ref[(4 * zh + zl) ^ COLUMN, 0:16, :] = quarters[zl % 2]
+            out_ref[(4 * zh + zl) ^ COLUMN, 16:32, :] = quarters[zl % 2 + 2]
+            out_ref[(4 * zh + zl) ^ COLUMN, 32:48, :] = tile
 
 
 def lay(flat_ref, pieces):
@@ -104,7 +104,7 @@
             out_ref[i, 16 * b : 16 * b + 16, :] = stepped
     update_ref[...] = moment_ref[zb, 0]
     for slot in range(12):
-        tile = column_ref[4 * (zh ^ (slot // 4 + 1) ^ COLUMN) + slot % 4, 32:48, :]
+        tile = column_ref[(4 * (zh ^ (slot // 4 + 1)) + slot % 4) ^ COLUMN, 32:48, :]
         for i in range(16):
             out_ref[i, 32 + 16 * slot : 48 + 16 * slot, :] = tile
 
@@ -123,7 +123,7 @@
             [pair_ref[q % 2, p, 16 * (q // 2) : 16 * (q // 2) + 16, :].astype(F32) for q in range(4)],
         )
         for k in range(9):
-            rows_ref[7 * (p ^ PLANE) : 7 * (p ^ PLANE) + 7, 128 * k : 128 * k + 128] = flat_ref[p, pl.ds(k, 7, stride=9), :]
+            rows_ref[7 * (p ^ SPREAD) : 7 * (p ^ SPREAD) + 7, 128 * k : 128 * k + 128] = flat_ref[p, pl.ds(k, 7, stride=9), :]
     out_ref[...] = rows_ref[...].astype(BF16)
 
 
@@ -136,7 +136,7 @@
                 low = pl.multiple_of(224 * (zh ^ d) + 112 * half + 16 * (t // 9), 16)
                 slot = 32 + 16 * (4 * (d - 1) + t % 4)
                 whole_ref[pl.ds(low, 16), 128 * (t % 9) : 128 * (t % 9) + 128] = ref[
-                    (t // 4) ^ PLANE, slot : slot + 16, :
+                    (t // 4) ^ SPREAD, slot : slot + 16, :
                 ]
     copies = []
     for i in range(3):
@@ -165,10 +165,11 @@
 
 def exchange(a, over):
     ids = np.arange(512).reshape(4, 2, 16, 4)
-    if over == "plane":
-        groups = ids[:, :, np.arange(16) ^ PLANE].transpose(0, 1, 3, 2).reshape(32, 16)
+    if over == "column":
+        groups = ids.transpose(1, 2, 0, 3).reshape(32, 16)[:, np.arange(16) ^ COLUMN]
     else:
-        groups = ids[np.arange(4) ^ COLUMN].transpose(1, 2, 0, 3).reshape(32, 16)
+        first = PLANE if over == "plane" else SPREAD
+        groups = ids[:, :, np.arange(16) ^ first].transpose(0, 1, 3, 2).reshape(32, 16)
     return lax.all_to_all(a, AXES, 0, 0, axis_index_groups=groups.tolist())
 
 
@@ -214,7 +215,7 @@
         [SMEM] * 2 + [VMEM] * 4,
         [pltpu.VMEM((2, 2, 16, 128), F32)],
     )
-    spread = exchange(spread, "plane")
+    spread = exchange(spread, "spread")
     others = lax.ppermute(spread, "core", [(0, 1), (1, 0)])
     half = call(stepped_kernel, shape((16, 32, 128), BF16), (spread,), [VMEM])
     other = lax.ppermute(half, "za", [(0, 1), (1, 0)])

time: 93.6 us -> 92.8 us (level)
  starting transfers between devices: 40.8 us -> 39.7 us
    all_to_all x2, starting transfers between devices: 22 us -> 20.2 us  [exchange(): return lax.all_to_all(a, AXES, 0, 0, axis_index_groups=groups.tolist())]
    all_to_all x2, waiting for transfers between devices: 13.5 us -> 14.5 us  [exchange(): return lax.all_to_all(a, AXES, 0, 0, axis_index_groups=groups.tolist())]
where the time goes in v6:
time: 92.8 us; the launch traced here: 92.3 us
  starting transfers between devices  39.7 us (43%)
  waiting for transfers between devices  19.7 us (21%)
  blocking collectives  19.2 us (21%)
  Pallas kernels  10.6 us (11%)
  local copies, waits for them, and re-layouts  2.16 us (2%)
    all_to_all x2, starting transfers between devices, exchange(): return lax.all_to_all(a, AXES, 0, 0, axis_index_groups=groups.tolist())  20.2 us
    all_to_all x1, blocking collectives, exchange(): return lax.all_to_all(a, AXES, 0, 0, axis_index_groups=groups.tolist())  19.2 us
    all_to_all x2, waiting for transfers between devices, exchange(): return lax.all_to_all(a, AXES, 0, 0, axis_index_groups=groups.tolist())  14.5 us
    pallas_call x9, Pallas kernels, call(): pl.pallas_call(kernel, out_shape=outs, in_specs=specs, out_specs=jax.tree...  10.6 us
    ppermute x1, starting transfers between devices, shards(): got = lax.ppermute(send, 'core', [(0, 1), (1, 0)])  8.79 us
    ppermute x1, waiting for transfers between devices, shards(): near = lax.ppermute(moments, 'zb', [(0, 1), (1, 0)])  3.68 us
    ppermute x1, starting transfers between devices, shards(): other = lax.ppermute(half, 'za', [(0, 1), (1, 0)])  3.29 us
    ppermute x1, starting transfers between devices, shards(): yours = lax.ppermute(mine, 'core', [(0, 1), (1, 0)])  2.84 us
  transfers between devices with their start and end apart: 7, of which 5 were waited for; matrix products, arithmetic and copies ran while one was open for 0% of the time, Pallas kernels for 5%

profile of v6, /device:TPU:1, one launch (start us, length us, event | category | flops | bytes accessed | tf_op | source)
XLA Modules:
  0.0 92.3 jit_solution(18439404629851794866)
XLA Ops:
  0.6 1.3 %copy-done.1 = bf16[768,896]{1,0:T(8,128)(2,1)S(1)} copy-done((bf16[768,896]{1,0:T(8,128)(2,1)S(1)}, bf16[768,896]{1,0:T(8,128)(2,1)}, u32[]{:S(2)}) %copy-start.1) | copy-done | bytes 1376280
  2.0 1.1 %shard_map.76.turned_ref = bf16[2,2,256,768]{3,2,1,0:T(8,128)(2,1)S(1)} custom-call(bf16[768,896]{1,0:T(8,128)(2,1)S(1)} %copy-done.1), custom_call_target="tpu_custom_call" | custom-call | tf_op jit(solution)/shard_map/pallas_call | solution.py:156
  3.0 0.4 copy-done
  3.5 1.2 %shard_map.78 = bf16[16,32,1152]{2,1,0:T(8,128)(2,1)S(1)} custom-call(s32[1]{0:T(128)S(6)} %sub.10.half_ref, bf16[2,2,256,768]{3,2,1,0:T(8,128)(2,1)S(1)} %shard_map.76.turned_ref, bf16[768,1152]{1,0:T(8,128)(2,1)S(1)} %copy-done), custom_call_target="tpu_custom_call" | custom-call | tf_op jit(solution)/shard_map/pallas_call | solution.py:156
  4.7 8.8 %collective-permute-start = (bf16[16,32,1152]{2,1,0:T(8,128)(2,1)S(1)}, bf16[16,32,1152]{2,1,0:T(8,128)(2,1)S(1)}, u32[]{:S(2)}, u32[]{:S(2)}) collective-permute-start(bf16[16,32,1152]{2,1,0:T(8,128)(2,1)S(1)} %shard_map.78), channel_id=1, source_target_pairs={{0,64},{64,0},{1,65},{65,1},{2,66},{66,2},{3,67},{67,3},{4,68},{68... | collective-permute-start | bytes 3538952 | tf_op jit(solution)/shard_map/ppermute | solution.py:188
  13.5 1.2 %shard_map.77.kept_ref = bf16[16,32,1152]{2,1,0:T(8,128)(2,1)S(1)} custom-call(s32[1]{0:T(128)} %bitcast.4.half_ref.core_ref, bf16[2,2,256,768]{3,2,1,0:T(8,128)(2,1)S(1)} %shard_map.76.turned_ref, bf16[768,1152]{1,0:T(8,128)(2,1)S(1)} %copy-done), custom_call_target="tpu_custom_call" | custom-call | tf_op jit(solution)/shard_map/pallas_call | solution.py:156
  14.7 1.2 %collective-permute-done.got_ref = bf16[16,32,1152]{2,1,0:T(8,128)(2,1)S(1)} collective-permute-done((bf16[16,32,1152]{2,1,0:T(8,128)(2,1)S(1)}, bf16[16,32,1152]{2,1,0:T(8,128)(2,1)S(1)}, u32[]{:S(2)}, u32[]{:S(2)}) %collective-permute-start) | collective-permute-done | bytes 1179680 | tf_op jit(solution)/shard_map/ppermute | solution.py:188
  15.9 1.2 %shard_map.79 = bf16[16,32,1152]{2,1,0:T(8,128)(2,1)} custom-call(bf16[16,32,1152]{2,1,0:T(8,128)(2,1)S(1)} %shard_map.77.kept_ref, bf16[16,32,1152]{2,1,0:T(8,128)(2,1)S(1)} %collective-permute-done.got_ref), custom_call_target="tpu_custom_call" | custom-call | tf_op jit(solution)/shard_map/pallas_call | solution.py:156
  17.1 6.8 %all-to-all-start = ((bf16[16,32,1152]{2,1,0:T(8,128)(2,1)}), bf16[16,32,1152]{2,1,0:T(8,128)(2,1)S(1)}, u32[]{:S(2)}, u32[]{:S(2)}) async-start(bf16[16,32,1152]{2,1,0:T(8,128)(2,1)} %shard_map.79), calls=%async_computation | async-start | bytes 2359296 | tf_op jit(solution)/shard_map/all_to_all | solution.py:173
  23.9 2.8 %collective-permute-start.1 = (bf16[112,1152]{1,0:T(8,128)(2,1)S(1)}, bf16[112,1152]{1,0:T(8,128)(2,1)S(1)}, u32[]{:S(2)}, u32[]{:S(2)}) collective-permute-start(bf16[112,1152]{1,0:T(8,128)(2,1)S(1)} %copy-done.2), channel_id=1, source_target_pairs={{0,64},{64,0},{1,65},{65,1},{2,66},{66,2},{3,67},{67,3},{4,68},{68... | collective-permute-start | bytes 774152 | tf_op jit(solution)/shard_map/ppermute | solution.py:201
  26.8 1.9 %collective-permute-start.2 = (f32[2,16,128]{2,1,0:T(8,128)S(1)}, f32[2,16,128]{2,1,0:T(8,128)S(1)}, u32[]{:S(2)}, u32[]{:S(2)}) collective-permute-start(f32[2,16,128]{2,1,0:T(8,128)S(1)} %pad_maximum_fusion.own_ref), channel_id=1, source_target_pairs={{0,2},{2,0},{1,3},{3,1},{4,6},{6,4},{5,7},{7,5},{8,10},{10,8},{9,1... | collective-permute-start | bytes 49160 | tf_op jit(solution)/shard_map/ppermute | solution.py:200
  28.8 3.7 %collective-permute-done.2.other_ref = f32[2,16,128]{2,1,0:T(8,128)S(1)} collective-permute-done((f32[2,16,128]{2,1,0:T(8,128)S(1)}, f32[2,16,128]{2,1,0:T(8,128)S(1)}, u32[]{:S(2)}, u32[]{:S(2)}) %collective-permute-start.2) | collective-permute-done | bytes 16416 | tf_op jit(solution)/shard_map/ppermute | solution.py:200
  32.5 5.7 %all-to-all-done.plane_ref = bf16[16,32,1152]{2,1,0:T(8,128)(2,1)S(1)} async-done(((bf16[16,32,1152]{2,1,0:T(8,128)(2,1)}), bf16[16,32,1152]{2,1,0:T(8,128)(2,1)S(1)}, u32[]{:S(2)}, u32[]{:S(2)}) %all-to-all-start) | async-done | bytes 1179680 | tf_op jit(solution)/shard_map/all_to_all | solution.py:173
  38.2 0.9 shard_map.80
  39.1 13.4 %all-to-all-start.1 = ((bf16[16,48,128]{2,1,0:T(8,128)(2,1)}), bf16[16,48,128]{2,1,0:T(8,128)(2,1)S(1)}, u32[]{:S(2)}, u32[]{:S(2)}) async-start(bf16[16,48,128]{2,1,0:T(8,128)(2,1)} %shard_map.80), calls=%async_computation.1 | async-start | bytes 393216 | tf_op jit(solution)/shard_map/all_to_all | solution.py:173
  52.5 0.3 reshape.27
  53.0 8.8 %all-to-all-done.1.column_ref = bf16[16,48,128]{2,1,0:T(8,128)(2,1)S(1)} async-done(((bf16[16,48,128]{2,1,0:T(8,128)(2,1)}), bf16[16,48,128]{2,1,0:T(8,128)(2,1)S(1)}, u32[]{:S(2)}, u32[]{:S(2)}) %all-to-all-start.1) | async-done | bytes 196640 | tf_op jit(solution)/shard_map/all_to_all | solution.py:173
  61.7 0.7 shard_map.81
  62.4 19.2 %all_to_all.15.spread_ref.own_ref = bf16[16,224,128]{2,1,0:T(8,128)(2,1)S(1)} all-to-all(bf16[16,224,128]{2,1,0:T(8,128)(2,1)S(1)} %get-tuple-element.19), channel_id=1, replica_groups={{40,44,32,36,56,60,48,52,8,12,0,4,24,28,16,20},{41,45,33,37,57,61,49,53..., dimensions={0} | all-to-all | bytes 1835008 | tf_op jit(solution)/shard_map/all_to_all | solution.py:173
  81.6 2.7 %collective-permute-start.4 = (bf16[16,224,128]{2,1,0:T(8,128)(2,1)S(1)}, bf16[16,224,128]{2,1,0:T(8,128)(2,1)S(1)}, u32[]{:S(2)}, u32[]{:S(2)}) collective-permute-start(bf16[16,224,128]{2,1,0:T(8,128)(2,1)S(1)} %all_to_all.15.spread_ref.own_ref), channel_id=1, source_target_pairs={{0,64},{64,0},{1,65},{65,1},{2,66},{66,2},{3,67},{67,3},{4,68},{68... | collective-permute-start | bytes 2752520 | tf_op jit(solution)/shard_map/ppermute | solution.py:219
  84.3 3.3 %collective-permute-start.3 = (bf16[16,32,128]{2,1,0:T(8,128)(2,1)S(1)}, bf16[16,32,128]{2,1,0:T(8,128)(2,1)S(1)}, u32[]{:S(2)}, u32[]{:S(2)}) collective-permute-start(bf16[16,32,128]{2,1,0:T(8,128)(2,1)S(1)} %shard_map.82.own_ref), channel_id=1, source_target_pairs={{0,1},{1,0},{2,3},{3,2},{4,5},{5,4},{6,7},{7,6},{8,9},{9,8},{10,11... | collective-permute-start | bytes 393224 | tf_op jit(solution)/shard_map/ppermute | solution.py:221
  87.6 3.3 %shard_map.83 = bf16[768,896]{1,0:T(8,128)(2,1)} custom-call(s32[1]{0:T(128)} %bitcast.4.half_ref.core_ref, s32[1]{0:T(128)} %bitcast.1.zh_ref, bf16[768,1152]{1,0:T(8,128)(2,1)S(1)} %copy-done, bf16[112,1152]{1,0:T(8,128)(2,1)S(1)} %copy-done.2, bf16[112,1152]{1,0:T(8,128)(2,1)S(1)} %collective-permute-done.1.yours_ref, ...), custom_call_target="tpu_custom_call" | custom-call | tf_op jit(solution)/shard_map/pallas_call | solution.py:156
  91.0 0.4 collective-permute-done.3.other_ref
  91.3 1.0 %shard_map.84 = bf16[112,1152]{1,0:T(8,128)(2,1)} custom-call(s32[1]{0:T(128)} %bitcast.8.za_ref, bf16[16,32,128]{2,1,0:T(8,128)(2,1)S(1)} %shard_map.82.own_ref, bf16[16,32,128]{2,1,0:T(8,128)(2,1)S(1)} %collective-permute-done.3.other_ref), custom_call_target="tpu_custom_call" | custom-call | tf_op jit(solution)/shard_map/pallas_call | solution.py:156
  (17 shorter events, 0.2 us)
Async XLA Ops:
  0.6 1.3 %copy-start.1 = (bf16[768,896]{1,0:T(8,128)(2,1)S(1)}, bf16[768,896]{1,0:T(8,128)(2,1)}, u32[]{:S(2)}) copy-start(bf16[768,896]{1,0:T(8,128)(2,1)} %x_ref.1) | copy-start | bytes 4128772
  2.0 1.5 %copy-start = (bf16[768,1152]{1,0:T(8,128)(2,1)S(1)}, bf16[768,1152]{1,0:T(8,128)(2,1)}, u32[]{:S(2)}) copy-start(bf16[768,1152]{1,0:T(8,128)(2,1)} %c_ref.5) | copy-start | bytes 5308420
  4.7 10.0 %copy-start.3 = (f32[2016]{0:T(1024)S(1)}, f32[2016]{0:T(1024)}, u32[]{:S(2)}) copy-start(f32[2016]{0:T(1024)} %param.9) | copy-start | bytes 24196
  4.7 10.0 %copy-start.4 = (f32[2016]{0:T(1024)S(1)}, f32[2016]{0:T(1024)}, u32[]{:S(2)}) copy-start(f32[2016]{0:T(1024)} %param.8) | copy-start | bytes 24196
  4.7 11.2 %collective-permute-start = (bf16[16,32,1152]{2,1,0:T(8,128)(2,1)S(1)}, bf16[16,32,1152]{2,1,0:T(8,128)(2,1)S(1)}, u32[]{:S(2)}, u32[]{:S(2)}) collective-permute-start(bf16[16,32,1152]{2,1,0:T(8,128)(2,1)S(1)} %shard_map.78), channel_id=1, source_target_pairs={{0,64},{64,0},{1,65},{65,1},{2,66},{66,2},{3,67},{67,3},{4,68},{68... | collective-permute-start | bytes 3538952 | tf_op jit(solution)/shard_map/ppermute | solution.py:188
  17.1 6.8 %copy-start.2 = (bf16[112,1152]{1,0:T(8,128)(2,1)S(1)}, bf16[112,1152]{1,0:T(8,128)(2,1)}, u32[]{:S(2)}) copy-start(bf16[112,1152]{1,0:T(8,128)(2,1)} %mine_ref.1) | copy-start | bytes 774148
  17.1 21.1 %all-to-all-start = ((bf16[16,32,1152]{2,1,0:T(8,128)(2,1)}), bf16[16,32,1152]{2,1,0:T(8,128)(2,1)S(1)}, u32[]{:S(2)}, u32[]{:S(2)}) async-start(bf16[16,32,1152]{2,1,0:T(8,128)(2,1)} %shard_map.79), calls=%async_computation | async-start | bytes 2359296 | tf_op jit(solution)/shard_map/all_to_all | solution.py:173
  23.9 8.5 %collective-permute-start.1 = (bf16[112,1152]{1,0:T(8,128)(2,1)S(1)}, bf16[112,1152]{1,0:T(8,128)(2,1)S(1)}, u32[]{:S(2)}, u32[]{:S(2)}) collective-permute-start(bf16[112,1152]{1,0:T(8,128)(2,1)S(1)} %copy-done.2), channel_id=1, source_target_pairs={{0,64},{64,0},{1,65},{65,1},{2,66},{66,2},{3,67},{67,3},{4,68},{68... | collective-permute-start | bytes 774152 | tf_op jit(solution)/shard_map/ppermute | solution.py:201
  26.8 5.7 %collective-permute-start.2 = (f32[2,16,128]{2,1,0:T(8,128)S(1)}, f32[2,16,128]{2,1,0:T(8,128)S(1)}, u32[]{:S(2)}, u32[]{:S(2)}) collective-permute-start(f32[2,16,128]{2,1,0:T(8,128)S(1)} %pad_maximum_fusion.own_ref), channel_id=1, source_target_pairs={{0,2},{2,0},{1,3},{3,1},{4,6},{6,4},{5,7},{7,5},{8,10},{10,8},{9,1... | collective-permute-start | bytes 49160 | tf_op jit(solution)/shard_map/ppermute | solution.py:200
  39.1 22.6 %all-to-all-start.1 = ((bf16[16,48,128]{2,1,0:T(8,128)(2,1)}), bf16[16,48,128]{2,1,0:T(8,128)(2,1)S(1)}, u32[]{:S(2)}, u32[]{:S(2)}) async-start(bf16[16,48,128]{2,1,0:T(8,128)(2,1)} %shard_map.80), calls=%async_computation.1 | async-start | bytes 393216 | tf_op jit(solution)/shard_map/all_to_all | solution.py:173
  81.6 6.0 %collective-permute-start.4 = (bf16[16,224,128]{2,1,0:T(8,128)(2,1)S(1)}, bf16[16,224,128]{2,1,0:T(8,128)(2,1)S(1)}, u32[]{:S(2)}, u32[]{:S(2)}) collective-permute-start(bf16[16,224,128]{2,1,0:T(8,128)(2,1)S(1)} %all_to_all.15.spread_ref.own_ref), channel_id=1, source_target_pairs={{0,64},{64,0},{1,65},{65,1},{2,66},{66,2},{3,67},{67,3},{4,68},{68... | collective-permute-start | bytes 2752520 | tf_op jit(solution)/shard_map/ppermute | solution.py:219
  84.3 7.0 %collective-permute-start.3 = (bf16[16,32,128]{2,1,0:T(8,128)(2,1)S(1)}, bf16[16,32,128]{2,1,0:T(8,128)(2,1)S(1)}, u32[]{:S(2)}, u32[]{:S(2)}) collective-permute-start(bf16[16,32,128]{2,1,0:T(8,128)(2,1)S(1)} %shard_map.82.own_ref), channel_id=1, source_target_pairs={{0,1},{1,0},{2,3},{3,2},{4,5},{5,4},{6,7},{7,6},{8,9},{9,8},{10,11... | collective-permute-start | bytes 393224 | tf_op jit(solution)/shard_map/ppermute | solution.py:221

commit v7 on v6

--- a/solution.py
+++ b/solution.py
@@ -51,8 +51,8 @@
             flat_ref[zh, pl.ds(k, 8, stride=9), :] = total[8 * zh : 8 * zh + 8, 128 * k : 128 * k + 128]
         quarters = [cut(flat_ref.at[zh], q).astype(BF16) for q in range(4)]
         for zl in range(4):
-            out_ref[(4 * zh + zl) ^ COLUMN, 0:16, :] = quarters[zl % 2]
-            out_ref[(4 * zh + zl) ^ COLUMN, 16:32, :] = quarters[zl % 2 + 2]
+            out_ref[(4 * zh + zl) ^ COLUMN, 0:16, :] = quarters[zl // 2 * 2]
+            out_ref[(4 * zh + zl) ^ COLUMN, 16:32, :] = quarters[zl // 2 * 2 + 1]
             out_ref[(4 * zh + zl) ^ COLUMN, 32:48, :] = tile
 
 
@@ -84,11 +84,11 @@
 
 
 def step_kernel(
-    zb_ref, zh_ref, column_ref, own_ref, other_ref, current_ref, update_ref, out_ref, moment_ref
+    za_ref, zh_ref, column_ref, own_ref, other_ref, current_ref, update_ref, out_ref, moment_ref
 ):
-    zb, zh = zb_ref[0], zh_ref[0]
-    moment_ref[zb] = own_ref[...]
-    moment_ref[1 - zb] = other_ref[...]
+    za, zh = za_ref[0], zh_ref[0]
+    moment_ref[za] = own_ref[...]
+    moment_ref[1 - za] = other_ref[...]
     for b in range(2):
         gradient = column_ref[0, 16 * b : 16 * b + 16, :].astype(F32)
         for i in range(1, 16):
@@ -102,7 +102,7 @@
         moment_ref[b, 0] = update
         for i in range(16):
             out_ref[i, 16 * b : 16 * b + 16, :] = stepped
-    update_ref[...] = moment_ref[zb, 0]
+    update_ref[...] = moment_ref[za, 0]
     for slot in range(12):
         tile = column_ref[(4 * (zh ^ (slot // 4 + 1)) + slot % 4) ^ COLUMN, 32:48, :]
         for i in range(16):
@@ -113,14 +113,14 @@
     out_ref[...] = spread_ref[:, 0:32, :]
 
 
-def rows_kernel(za_ref, own_ref, other_ref, out_ref, pair_ref, flat_ref, rows_ref):
-    za = za_ref[0]
-    pair_ref[za] = own_ref[...]
-    pair_ref[1 - za] = other_ref[...]
+def rows_kernel(zb_ref, own_ref, other_ref, out_ref, pair_ref, flat_ref, rows_ref):
+    zb = zb_ref[0]
+    pair_ref[zb] = own_ref[...]
+    pair_ref[1 - zb] = other_ref[...]
     for p in range(16):
         lay(
             flat_ref.at[p],
-            [pair_ref[q % 2, p, 16 * (q // 2) : 16 * (q // 2) + 16, :].astype(F32) for q in range(4)],
+            [pair_ref[q // 2, p, 16 * (q % 2) : 16 * (q % 2) + 16, :].astype(F32) for q in range(4)],
         )
         for k in range(9):
             rows_ref[7 * (p ^ SPREAD) : 7 * (p ^ SPREAD) + 7, 128 * k : 128 * k + 128] = flat_ref[p, pl.ds(k, 7, stride=9), :]
@@ -191,13 +191,13 @@
     own_tile = jnp.minimum(own, 62)
     tile = lax.dynamic_slice(weight, (16 * (own_tile // 9), 128 * (own_tile % 9)), (16, 128))
     flat = weight.reshape(-1)
-    pair = own // 4 * 4 + lax.axis_index("za")
-    current = [lax.dynamic_slice_in_dim(flat, (pair + 2 * b) * 2016, 2016, 0).astype(F32) for b in range(2)]
+    pair = own // 2 * 2
+    current = [lax.dynamic_slice_in_dim(flat, (pair + b) * 2016, 2016, 0).astype(F32) for b in range(2)]
     current = jnp.stack([jnp.pad(a, (0, 32)).reshape(16, 128) for a in current])
     moments = jnp.stack([jnp.pad(a, (0, 32)).reshape(16, 128) for a in (moment_one, moment_two)])
     moments, mine, chip = lax.optimization_barrier((moments, weight, chip))
     plane = exchange(chip, "plane")
-    near = lax.ppermute(moments, "zb", [(0, 1), (1, 0)])
+    near = lax.ppermute(moments, "za", [(0, 1), (1, 0)])
     yours = lax.ppermute(mine, "core", [(0, 1), (1, 0)])
     plane, yours, near = lax.optimization_barrier((plane, yours, near))
     column = call(
@@ -211,14 +211,14 @@
     update, spread = call(
         step_kernel,
         (shape((16, 128), F32), shape((16, 224, 128), BF16)),
-        (zb, zh, column, moments, near, current),
+        (za, zh, column, moments, near, current),
         [SMEM] * 2 + [VMEM] * 4,
         [pltpu.VMEM((2, 2, 16, 128), F32)],
     )
     spread = exchange(spread, "spread")
     others = lax.ppermute(spread, "core", [(0, 1), (1, 0)])
     half = call(stepped_kernel, shape((16, 32, 128), BF16), (spread,), [VMEM])
-    other = lax.ppermute(half, "za", [(0, 1), (1, 0)])
+    other = lax.ppermute(half, "zb", [(0, 1), (1, 0)])
     grad_in = call(
         input_kernel,
         shape((768, 896), BF16),
@@ -235,7 +235,7 @@
     new_weight = call(
         rows_kernel,
         shape((112, 1152), BF16),
-        (za, half, other),
+        (zb, half, other),
         [SMEM, VMEM, VMEM],
         [pltpu.VMEM((2, 16, 32, 128), BF16), pltpu.VMEM((16, 72, 128), F32), pltpu.VMEM((112, 1152), F32)],
     )

time: 92.8 us -> 96.5 us (1.040)
  waiting for transfers between devices: 19.7 us -> 24.2 us
    ppermute x2, waiting for transfers between devices: 4.03 us -> 7.58 us  [the longest x1 4.79 us: shards(): other = lax.ppermute(half, 'zb', [(0, 1), (1, 0)])]
where the time goes in v7:
time: 96.5 us; the launch traced here: 96 us
  starting transfers between devices  39 us (40%)
  waiting for transfers between devices  24.2 us (25%)
  blocking collectives  19.2 us (20%)
  Pallas kernels  10.6 us (11%)
  local copies, waits for them, and re-layouts  2.16 us (2%)
    all_to_all x2, starting transfers between devices, exchange(): return lax.all_to_all(a, AXES, 0, 0, axis_index_groups=groups.tolist())  20.2 us
    all_to_all x1, blocking collectives, exchange(): return lax.all_to_all(a, AXES, 0, 0, axis_index_groups=groups.tolist())  19.2 us
    all_to_all x2, waiting for transfers between devices, exchange(): return lax.all_to_all(a, AXES, 0, 0, axis_index_groups=groups.tolist())  15.4 us
    pallas_call x9, Pallas kernels, call(): pl.pallas_call(kernel, out_shape=outs, in_specs=specs, out_specs=jax.tree...  10.6 us
    ppermute x1, starting transfers between devices, shards(): got = lax.ppermute(send, 'core', [(0, 1), (1, 0)])  8.79 us
    ppermute x1, waiting for transfers between devices, shards(): other = lax.ppermute(half, 'zb', [(0, 1), (1, 0)])  4.79 us
    ppermute x1, starting transfers between devices, shards(): yours = lax.ppermute(mine, 'core', [(0, 1), (1, 0)])  2.84 us
    ppermute x1, waiting for transfers between devices, shards(): near = lax.ppermute(moments, 'za', [(0, 1), (1, 0)])  2.78 us
  transfers between devices with their start and end apart: 7, of which 5 were waited for; matrix products, arithmetic and copies ran while one was open for 0% of the time, Pallas kernels for 5%

profile of v7, /device:TPU:1, one launch (start us, length us, event | category | flops | bytes accessed | tf_op | source)
XLA Modules:
  0.0 96.0 jit_solution(271630996459240155)
XLA Ops:
  0.6 1.3 %copy-done.1 = bf16[768,896]{1,0:T(8,128)(2,1)S(1)} copy-done((bf16[768,896]{1,0:T(8,128)(2,1)S(1)}, bf16[768,896]{1,0:T(8,128)(2,1)}, u32[]{:S(2)}) %copy-start.1) | copy-done | bytes 1376280
  2.0 1.1 %shard_map.76.turned_ref = bf16[2,2,256,768]{3,2,1,0:T(8,128)(2,1)S(1)} custom-call(bf16[768,896]{1,0:T(8,128)(2,1)S(1)} %copy-done.1), custom_call_target="tpu_custom_call" | custom-call | tf_op jit(solution)/shard_map/pallas_call | solution.py:156
  3.0 0.4 copy-done
  3.5 1.2 %shard_map.78 = bf16[16,32,1152]{2,1,0:T(8,128)(2,1)S(1)} custom-call(s32[1]{0:T(128)S(6)} %sub.10.half_ref, bf16[2,2,256,768]{3,2,1,0:T(8,128)(2,1)S(1)} %shard_map.76.turned_ref, bf16[768,1152]{1,0:T(8,128)(2,1)S(1)} %copy-done), custom_call_target="tpu_custom_call" | custom-call | tf_op jit(solution)/shard_map/pallas_call | solution.py:156
  4.7 8.8 %collective-permute-start = (bf16[16,32,1152]{2,1,0:T(8,128)(2,1)S(1)}, bf16[16,32,1152]{2,1,0:T(8,128)(2,1)S(1)}, u32[]{:S(2)}, u32[]{:S(2)}) collective-permute-start(bf16[16,32,1152]{2,1,0:T(8,128)(2,1)S(1)} %shard_map.78), channel_id=1, source_target_pairs={{0,64},{64,0},{1,65},{65,1},{2,66},{66,2},{3,67},{67,3},{4,68},{68... | collective-permute-start | bytes 3538952 | tf_op jit(solution)/shard_map/ppermute | solution.py:188
  13.5 1.2 %shard_map.77.kept_ref = bf16[16,32,1152]{2,1,0:T(8,128)(2,1)S(1)} custom-call(s32[1]{0:T(128)} %bitcast.4.half_ref.core_ref, bf16[2,2,256,768]{3,2,1,0:T(8,128)(2,1)S(1)} %shard_map.76.turned_ref, bf16[768,1152]{1,0:T(8,128)(2,1)S(1)} %copy-done), custom_call_target="tpu_custom_call" | custom-call | tf_op jit(solution)/shard_map/pallas_call | solution.py:156
  14.7 1.2 %collective-permute-done.got_ref = bf16[16,32,1152]{2,1,0:T(8,128)(2,1)S(1)} collective-permute-done((bf16[16,32,1152]{2,1,0:T(8,128)(2,1)S(1)}, bf16[16,32,1152]{2,1,0:T(8,128)(2,1)S(1)}, u32[]{:S(2)}, u32[]{:S(2)}) %collective-permute-start) | collective-permute-done | bytes 1179680 | tf_op jit(solution)/shard_map/ppermute | solution.py:188
  15.9 1.2 %shard_map.79 = bf16[16,32,1152]{2,1,0:T(8,128)(2,1)} custom-call(bf16[16,32,1152]{2,1,0:T(8,128)(2,1)S(1)} %shard_map.77.kept_ref, bf16[16,32,1152]{2,1,0:T(8,128)(2,1)S(1)} %collective-permute-done.got_ref), custom_call_target="tpu_custom_call" | custom-call | tf_op jit(solution)/shard_map/pallas_call | solution.py:156
  17.1 6.8 %all-to-all-start = ((bf16[16,32,1152]{2,1,0:T(8,128)(2,1)}), bf16[16,32,1152]{2,1,0:T(8,128)(2,1)S(1)}, u32[]{:S(2)}, u32[]{:S(2)}) async-start(bf16[16,32,1152]{2,1,0:T(8,128)(2,1)} %shard_map.79), calls=%async_computation | async-start | bytes 2359296 | tf_op jit(solution)/shard_map/all_to_all | solution.py:173
  23.9 2.8 %collective-permute-start.1 = (bf16[112,1152]{1,0:T(8,128)(2,1)S(1)}, bf16[112,1152]{1,0:T(8,128)(2,1)S(1)}, u32[]{:S(2)}, u32[]{:S(2)}) collective-permute-start(bf16[112,1152]{1,0:T(8,128)(2,1)S(1)} %copy-done.2), channel_id=1, source_target_pairs={{0,64},{64,0},{1,65},{65,1},{2,66},{66,2},{3,67},{67,3},{4,68},{68... | collective-permute-start | bytes 774152 | tf_op jit(solution)/shard_map/ppermute | solution.py:201
  26.8 1.9 %collective-permute-start.2 = (f32[2,16,128]{2,1,0:T(8,128)S(1)}, f32[2,16,128]{2,1,0:T(8,128)S(1)}, u32[]{:S(2)}, u32[]{:S(2)}) collective-permute-start(f32[2,16,128]{2,1,0:T(8,128)S(1)} %pad_maximum_fusion.own_ref), channel_id=1, source_target_pairs={{0,1},{1,0},{2,3},{3,2},{4,5},{5,4},{6,7},{7,6},{8,9},{9,8},{10,11... | collective-permute-start | bytes 49160 | tf_op jit(solution)/shard_map/ppermute | solution.py:200
  28.8 2.8 %collective-permute-done.2.other_ref = f32[2,16,128]{2,1,0:T(8,128)S(1)} collective-permute-done((f32[2,16,128]{2,1,0:T(8,128)S(1)}, f32[2,16,128]{2,1,0:T(8,128)S(1)}, u32[]{:S(2)}, u32[]{:S(2)}) %collective-permute-start.2) | collective-permute-done | bytes 16416 | tf_op jit(solution)/shard_map/ppermute | solution.py:200
  31.6 6.6 %all-to-all-done.plane_ref = bf16[16,32,1152]{2,1,0:T(8,128)(2,1)S(1)} async-done(((bf16[16,32,1152]{2,1,0:T(8,128)(2,1)}), bf16[16,32,1152]{2,1,0:T(8,128)(2,1)S(1)}, u32[]{:S(2)}, u32[]{:S(2)}) %all-to-all-start) | async-done | bytes 1179680 | tf_op jit(solution)/shard_map/all_to_all | solution.py:173
  38.2 0.9 shard_map.80
  39.1 13.4 %all-to-all-start.1 = ((bf16[16,48,128]{2,1,0:T(8,128)(2,1)}), bf16[16,48,128]{2,1,0:T(8,128)(2,1)S(1)}, u32[]{:S(2)}, u32[]{:S(2)}) async-start(bf16[16,48,128]{2,1,0:T(8,128)(2,1)} %shard_map.80), calls=%async_computation.1 | async-start | bytes 393216 | tf_op jit(solution)/shard_map/all_to_all | solution.py:173
  52.5 0.3 reshape.27
  52.9 8.8 %all-to-all-done.1.column_ref = bf16[16,48,128]{2,1,0:T(8,128)(2,1)S(1)} async-done(((bf16[16,48,128]{2,1,0:T(8,128)(2,1)}), bf16[16,48,128]{2,1,0:T(8,128)(2,1)S(1)}, u32[]{:S(2)}, u32[]{:S(2)}) %all-to-all-start.1) | async-done | bytes 196640 | tf_op jit(solution)/shard_map/all_to_all | solution.py:173
  61.7 0.7 shard_map.81
  62.4 19.2 %all_to_all.15.spread_ref.own_ref = bf16[16,224,128]{2,1,0:T(8,128)(2,1)S(1)} all-to-all(bf16[16,224,128]{2,1,0:T(8,128)(2,1)S(1)} %get-tuple-element.19), channel_id=1, replica_groups={{40,44,32,36,56,60,48,52,8,12,0,4,24,28,16,20},{41,45,33,37,57,61,49,53..., dimensions={0} | all-to-all | bytes 1835008 | tf_op jit(solution)/shard_map/all_to_all | solution.py:173
  81.6 2.7 %collective-permute-start.4 = (bf16[16,224,128]{2,1,0:T(8,128)(2,1)S(1)}, bf16[16,224,128]{2,1,0:T(8,128)(2,1)S(1)}, u32[]{:S(2)}, u32[]{:S(2)}) collective-permute-start(bf16[16,224,128]{2,1,0:T(8,128)(2,1)S(1)} %all_to_all.15.spread_ref.own_ref), channel_id=1, source_target_pairs={{0,64},{64,0},{1,65},{65,1},{2,66},{66,2},{3,67},{67,3},{4,68},{68... | collective-permute-start | bytes 2752520 | tf_op jit(solution)/shard_map/ppermute | solution.py:219
  84.3 2.6 %collective-permute-start.3 = (bf16[16,32,128]{2,1,0:T(8,128)(2,1)S(1)}, bf16[16,32,128]{2,1,0:T(8,128)(2,1)S(1)}, u32[]{:S(2)}, u32[]{:S(2)}) collective-permute-start(bf16[16,32,128]{2,1,0:T(8,128)(2,1)S(1)} %shard_map.82.own_ref), channel_id=1, source_target_pairs={{0,2},{2,0},{1,3},{3,1},{4,6},{6,4},{5,7},{7,5},{8,10},{10,8},{9,1... | collective-permute-start | bytes 393224 | tf_op jit(solution)/shard_map/ppermute | solution.py:221
  86.9 3.3 %shard_map.83 = bf16[768,896]{1,0:T(8,128)(2,1)} custom-call(s32[1]{0:T(128)} %bitcast.4.half_ref.core_ref, s32[1]{0:T(128)} %bitcast.1.zh_ref, bf16[768,1152]{1,0:T(8,128)(2,1)S(1)} %copy-done, bf16[112,1152]{1,0:T(8,128)(2,1)S(1)} %copy-done.2, bf16[112,1152]{1,0:T(8,128)(2,1)S(1)} %collective-permute-done.1.yours_ref, ...), custom_call_target="tpu_custom_call" | custom-call | tf_op jit(solution)/shard_map/pallas_call | solution.py:156
  90.3 4.8 %collective-permute-done.3.other_ref = bf16[16,32,128]{2,1,0:T(8,128)(2,1)S(1)} collective-permute-done((bf16[16,32,128]{2,1,0:T(8,128)(2,1)S(1)}, bf16[16,32,128]{2,1,0:T(8,128)(2,1)S(1)}, u32[]{:S(2)}, u32[]{:S(2)}) %collective-permute-start.3) | collective-permute-done | bytes 131104 | tf_op jit(solution)/shard_map/ppermute | solution.py:221
  95.0 1.0 shard_map.84
  (17 shorter events, 0.2 us)
Async XLA Ops:
  0.6 1.3 %copy-start.1 = (bf16[768,896]{1,0:T(8,128)(2,1)S(1)}, bf16[768,896]{1,0:T(8,128)(2,1)}, u32[]{:S(2)}) copy-start(bf16[768,896]{1,0:T(8,128)(2,1)} %x_ref.1) | copy-start | bytes 4128772
  2.0 1.5 %copy-start = (bf16[768,1152]{1,0:T(8,128)(2,1)S(1)}, bf16[768,1152]{1,0:T(8,128)(2,1)}, u32[]{:S(2)}) copy-start(bf16[768,1152]{1,0:T(8,128)(2,1)} %c_ref.5) | copy-start | bytes 5308420
  4.7 10.0 %copy-start.3 = (f32[2016]{0:T(1024)S(1)}, f32[2016]{0:T(1024)}, u32[]{:S(2)}) copy-start(f32[2016]{0:T(1024)} %param.9) | copy-start | bytes 24196
  4.7 10.0 %copy-start.4 = (f32[2016]{0:T(1024)S(1)}, f32[2016]{0:T(1024)}, u32[]{:S(2)}) copy-start(f32[2016]{0:T(1024)} %param.8) | copy-start | bytes 24196
  4.7 11.2 %collective-permute-start = (bf16[16,32,1152]{2,1,0:T(8,128)(2,1)S(1)}, bf16[16,32,1152]{2,1,0:T(8,128)(2,1)S(1)}, u32[]{:S(2)}, u32[]{:S(2)}) collective-permute-start(bf16[16,32,1152]{2,1,0:T(8,128)(2,1)S(1)} %shard_map.78), channel_id=1, source_target_pairs={{0,64},{64,0},{1,65},{65,1},{2,66},{66,2},{3,67},{67,3},{4,68},{68... | collective-permute-start | bytes 3538952 | tf_op jit(solution)/shard_map/ppermute | solution.py:188
  17.1 6.8 %copy-start.2 = (bf16[112,1152]{1,0:T(8,128)(2,1)S(1)}, bf16[112,1152]{1,0:T(8,128)(2,1)}, u32[]{:S(2)}) copy-start(bf16[112,1152]{1,0:T(8,128)(2,1)} %mine_ref.1) | copy-start | bytes 774148
  17.1 21.1 %all-to-all-start = ((bf16[16,32,1152]{2,1,0:T(8,128)(2,1)}), bf16[16,32,1152]{2,1,0:T(8,128)(2,1)S(1)}, u32[]{:S(2)}, u32[]{:S(2)}) async-start(bf16[16,32,1152]{2,1,0:T(8,128)(2,1)} %shard_map.79), calls=%async_computation | async-start | bytes 2359296 | tf_op jit(solution)/shard_map/all_to_all | solution.py:173
  23.9 7.6 %collective-permute-start.1 = (bf16[112,1152]{1,0:T(8,128)(2,1)S(1)}, bf16[112,1152]{1,0:T(8,128)(2,1)S(1)}, u32[]{:S(2)}, u32[]{:S(2)}) collective-permute-start(bf16[112,1152]{1,0:T(8,128)(2,1)S(1)} %copy-done.2), channel_id=1, source_target_pairs={{0,64},{64,0},{1,65},{65,1},{2,66},{66,2},{3,67},{67,3},{4,68},{68... | collective-permute-start | bytes 774152 | tf_op jit(solution)/shard_map/ppermute | solution.py:201
  26.8 4.8 %collective-permute-start.2 = (f32[2,16,128]{2,1,0:T(8,128)S(1)}, f32[2,16,128]{2,1,0:T(8,128)S(1)}, u32[]{:S(2)}, u32[]{:S(2)}) collective-permute-start(f32[2,16,128]{2,1,0:T(8,128)S(1)} %pad_maximum_fusion.own_ref), channel_id=1, source_target_pairs={{0,1},{1,0},{2,3},{3,2},{4,5},{5,4},{6,7},{7,6},{8,9},{9,8},{10,11... | collective-permute-start | bytes 49160 | tf_op jit(solution)/shard_map/ppermute | solution.py:200
  39.1 22.6 %all-to-all-start.1 = ((bf16[16,48,128]{2,1,0:T(8,128)(2,1)}), bf16[16,48,128]{2,1,0:T(8,128)(2,1)S(1)}, u32[]{:S(2)}, u32[]{:S(2)}) async-start(bf16[16,48,128]{2,1,0:T(8,128)(2,1)} %shard_map.80), calls=%async_computation.1 | async-start | bytes 393216 | tf_op jit(solution)/shard_map/all_to_all | solution.py:173
  81.6 5.3 %collective-permute-start.4 = (bf16[16,224,128]{2,1,0:T(8,128)(2,1)S(1)}, bf16[16,224,128]{2,1,0:T(8,128)(2,1)S(1)}, u32[]{:S(2)}, u32[]{:S(2)}) collective-permute-start(bf16[16,224,128]{2,1,0:T(8,128)(2,1)S(1)} %all_to_all.15.spread_ref.own_ref), channel_id=1, source_target_pairs={{0,64},{64,0},{1,65},{65,1},{2,66},{66,2},{3,67},{67,3},{4,68},{68... | collective-permute-start | bytes 2752520 | tf_op jit(solution)/shard_map/ppermute | solution.py:219
  84.3 10.7 %collective-permute-start.3 = (bf16[16,32,128]{2,1,0:T(8,128)(2,1)S(1)}, bf16[16,32,128]{2,1,0:T(8,128)(2,1)S(1)}, u32[]{:S(2)}, u32[]{:S(2)}) collective-permute-start(bf16[16,32,128]{2,1,0:T(8,128)(2,1)S(1)} %shard_map.82.own_ref), channel_id=1, source_target_pairs={{0,2},{2,0},{1,3},{3,1},{4,6},{6,4},{5,7},{7,5},{8,10},{10,8},{9,1... | collective-permute-start | bytes 393224 | tf_op jit(solution)/shard_map/ppermute | solution.py:221
